TPU v7x, 256 devices: a whole 4x4x8 slice. The times are simulated.
256 devices in a mesh: seq: 32 (over z, x_hi, core), dp: 8 (over y, x_lo).
Axes of the slice: x: 4 (x_hi: 2, x_lo: 2; x = x_hi * 2 + x_lo), y: 4, z: 8, core: 2. Of those that a mesh axis runs over, the one named last changes fastest.
Arguments:
- counts: int32 [8, 4096, 64], P('dp', 'seq'), may hold values from 0 to 63
- w_in: bfloat16 [64, 2304], replicated, may hold values from -0.75 to 0.75
- bias_one: float32 [768], replicated, may hold values from -4 to 4
- bias_two: float32 [768], replicated, may hold values from -4 to 4
- filter_one: bfloat16 [768, 4096], P('seq', 'dp'), may hold values from -0.09375 to 0.09375
- filter_two: bfloat16 [768, 4096], P('seq', 'dp'), may hold values from -0.09375 to 0.09375
- cotangent: bfloat16 [8, 768, 4096], P('dp', None, 'seq'), may hold values from -6 to 6
Outputs:
- output: bfloat16 [8, 768, 4096], P('dp', None, 'seq')
- grad_w_in: float32 [64, 2304], replicated
- grad_bias_one: float32 [768], replicated
- grad_bias_two: float32 [768], replicated
- grad_filter_one: bfloat16 [768, 4096], P(('seq', 'dp'))
- grad_filter_two: bfloat16 [768, 4096], P(('seq', 'dp'))
All inputs are finite; a program needn't handle non-finite values.
Results may differ from a plain program's by a relative error of at most 0.01.
Values may be sent and summed in bfloat16 or wider, within the bound.
A program may use at most 64 MiB of HBM per device.

v0:
```python
import math

import jax
import jax.numpy as jnp
from jax import lax
from jax.sharding import PartitionSpec as P

count_shift = 3.0
two_pi = 2.0 * math.pi
tile_len = 128
highest = lax.Precision.HIGHEST


def phase(left_side, right_side, modulus):
    product = left_side * right_side % modulus
    return product.astype(jnp.float32) * (two_pi / modulus)


def rotate(spectral, padded_len, sign):
    grid_shape = spectral.shape[2:]
    frequency = lax.broadcasted_iota(jnp.int32, grid_shape, 0)
    position = lax.broadcasted_iota(jnp.int32, grid_shape, 1)
    angles = phase(frequency, position, padded_len)
    cosine = jnp.cos(angles)
    sine_part = sign * jnp.sin(angles)
    real_part = spectral[:, 0]
    imag_part = spectral[:, 1]
    return jnp.stack(
        [real_part * cosine - imag_part * sine_part, real_part * sine_part + imag_part * cosine],
        axis=1,
    )


def transform(signal):
    channels, bin_total = signal.shape
    padded_len = 2 * bin_total
    row_count = padded_len // tile_len
    half_rows = row_count // 2
    blocks = signal.astype(jnp.float32).reshape(channels, half_rows, tile_len)
    frequency = lax.broadcasted_iota(jnp.int32, (row_count, half_rows), 0)
    position = lax.broadcasted_iota(jnp.int32, (row_count, half_rows), 1)
    angles = phase(frequency, position, row_count)
    first_table = jnp.stack([jnp.cos(angles), -jnp.sin(angles)], axis=0)
    partial_spec = jnp.einsum("rka,cab->crkb", first_table, blocks, precision=highest)
    turned = rotate(partial_spec, padded_len, -1.0)
    frequency = lax.broadcasted_iota(jnp.int32, (tile_len, tile_len), 0)
    position = lax.broadcasted_iota(jnp.int32, (tile_len, tile_len), 1)
    angles = phase(frequency, position, tile_len)
    cosine = jnp.cos(angles)
    sine_part = jnp.sin(angles)
    second_table = jnp.stack(
        [jnp.stack([cosine, sine_part], axis=1), jnp.stack([-sine_part, cosine], axis=1)], axis=0
    )
    return jnp.einsum("rksb,csjb->crjk", second_table, turned, precision=highest)


def untransform(spectral):
    row_count = spectral.shape[2]
    padded_len = row_count * tile_len
    half_rows = row_count // 2
    position = lax.broadcasted_iota(jnp.int32, (tile_len, tile_len), 0)
    frequency = lax.broadcasted_iota(jnp.int32, (tile_len, tile_len), 1)
    angles = phase(position, frequency, tile_len)
    cosine = jnp.cos(angles)
    sine_part = jnp.sin(angles)
    back_table = jnp.stack(
        [jnp.stack([cosine, -sine_part], axis=1), jnp.stack([sine_part, cosine], axis=1)], axis=0
    )
    reverted = jnp.einsum("rbsk,csjk->crjb", back_table, spectral, precision=highest)
    turned = rotate(reverted, padded_len, 1.0)
    position = lax.broadcasted_iota(jnp.int32, (half_rows, row_count), 0)
    frequency = lax.broadcasted_iota(jnp.int32, (half_rows, row_count), 1)
    angles = phase(position, frequency, row_count)
    last_table = jnp.stack([jnp.cos(angles), -jnp.sin(angles)], axis=1) / padded_len
    signal = jnp.einsum("ask,cskb->cab", last_table, turned, precision=highest)
    return signal.reshape(signal.shape[0], half_rows * tile_len)


def spec_product(left_side, right_side):
    real_left = left_side[:, 0]
    imag_left = left_side[:, 1]
    real_right = right_side[:, 0]
    imag_right = right_side[:, 1]
    return jnp.stack(
        [
            real_left * real_right - imag_left * imag_right,
            real_left * imag_right + imag_left * real_right,
        ],
        axis=1,
    )


def conj_product(left_side, right_side):
    real_left = left_side[:, 0]
    imag_left = left_side[:, 1]
    real_right = right_side[:, 0]
    imag_right = right_side[:, 1]
    return jnp.stack(
        [
            real_left * real_right + imag_left * imag_right,
            real_left * imag_right - imag_left * real_right,
        ],
        axis=1,
    )


def to_columns(block):
    seq_count = lax.axis_size("seq")
    group_width = block.shape[0] // seq_count
    arrived = lax.all_to_all(
        block.reshape(seq_count, group_width, block.shape[1]),
        "seq",
        split_axis=0,
        concat_axis=2,
        tiled=True,
    )
    return arrived.reshape(group_width, seq_count * block.shape[1])


def to_bins(block):
    arrived = lax.all_to_all(
        block.reshape(1, block.shape[0], block.shape[1]),
        "seq",
        split_axis=2,
        concat_axis=0,
        tiled=True,
    )
    return arrived.reshape(arrived.shape[0] * arrived.shape[1], arrived.shape[2])


def body(counts, w_in, bias_one, bias_two, filter_one, filter_two, cotangent):
    member_count = lax.axis_size("dp")
    seq_count = lax.axis_size("seq")
    length = counts.shape[1]
    channels = bias_one.shape[0]
    group_width = channels // seq_count
    bin_total = length * seq_count
    loss_scale = 1.0 / math.sqrt(member_count * bin_total)
    levels = (jnp.log1p(counts[0].astype(jnp.float32)) - count_shift).astype(jnp.bfloat16)
    projected = lax.dot_general(
        w_in, levels, (((0,), (1,)), ((), ())), preferred_element_type=jnp.float32
    )
    value_part = projected[:channels].astype(jnp.bfloat16)
    gate_one = projected[channels : 2 * channels].astype(jnp.bfloat16)
    gate_two = projected[2 * channels :].astype(jnp.bfloat16)
    rows_one, rows_two = (
        lax.all_gather(filter_one, "dp", axis=1, tiled=True),
        lax.all_gather(filter_two, "dp", axis=1, tiled=True),
    )
    filter_hat = transform(jnp.concatenate([rows_one, rows_two], axis=0))
    hat_one = filter_hat[:group_width]
    hat_two = filter_hat[group_width:]
    value_hat = transform(to_columns(value_part))
    conv_one = to_bins(untransform(spec_product(hat_one, value_hat)).astype(jnp.bfloat16))
    mixed_one = conv_one.astype(jnp.float32) + bias_one[:, None] * value_part.astype(jnp.float32)
    hidden = (gate_one.astype(jnp.float32) * mixed_one).astype(jnp.bfloat16)
    hidden_hat = transform(to_columns(hidden))
    conv_two = to_bins(untransform(spec_product(hat_two, hidden_hat)).astype(jnp.bfloat16))
    mixed_two = conv_two.astype(jnp.float32) + bias_two[:, None] * hidden.astype(jnp.float32)
    output = (gate_two.astype(jnp.float32) * mixed_two).astype(jnp.bfloat16)
    upstream = cotangent[0].astype(jnp.float32) * loss_scale
    grad_mixed_two = (upstream * gate_two.astype(jnp.float32)).astype(jnp.bfloat16)
    grad_two_hat = transform(to_columns(grad_mixed_two))
    carried_two = to_bins(untransform(conj_product(hat_two, grad_two_hat)).astype(jnp.bfloat16))
    grad_hidden = bias_two[:, None] * grad_mixed_two.astype(jnp.float32) + carried_two.astype(
        jnp.float32
    )
    grad_mixed_one = (grad_hidden * gate_one.astype(jnp.float32)).astype(jnp.bfloat16)
    grad_one_hat = transform(to_columns(grad_mixed_one))
    carried_one = to_bins(untransform(conj_product(hat_one, grad_one_hat)).astype(jnp.bfloat16))
    grad_value = bias_one[:, None] * grad_mixed_one.astype(jnp.float32) + carried_one.astype(
        jnp.float32
    )
    grad_projected = jnp.concatenate(
        [grad_value, grad_hidden * mixed_one, upstream * mixed_two], axis=0
    ).astype(jnp.bfloat16)
    bias_one_term = jnp.sum(
        grad_mixed_one.astype(jnp.float32) * value_part.astype(jnp.float32), axis=1
    )
    bias_two_term = jnp.sum(grad_mixed_two.astype(jnp.float32) * hidden.astype(jnp.float32), axis=1)
    weight_term = lax.dot_general(
        levels, grad_projected, (((0,), (1,)), ((), ())), preferred_element_type=jnp.float32
    )
    grad_weight, grad_bias_one, grad_bias_two = lax.psum(
        (weight_term, bias_one_term, bias_two_term), ("seq", "dp")
    )
    filter_terms = jnp.stack(
        [conj_product(value_hat, grad_one_hat), conj_product(hidden_hat, grad_two_hat)], axis=0
    )
    signals = untransform(
        filter_terms.reshape((2 * group_width,) + filter_terms.shape[2:])
    ).reshape(2, group_width, bin_total)
    filter_grads = lax.psum_scatter(signals, "dp", scatter_dimension=1, tiled=True)
    return (
        output[None],
        grad_weight,
        grad_bias_one,
        grad_bias_two,
        filter_grads[0].astype(jnp.bfloat16),
        filter_grads[1].astype(jnp.bfloat16),
    )


def solution(mesh):
    return jax.shard_map(
        body,
        mesh=mesh,
        in_specs=(
            P("dp", "seq", None),
            P(),
            P(),
            P(),
            P("seq", "dp"),
            P("seq", "dp"),
            P("dp", None, "seq"),
        ),
        out_specs=(
            P("dp", None, "seq"),
            P(),
            P(),
            P(),
            P(("seq", "dp"), None),
            P(("seq", "dp"), None),
        ),
        check_vma=False,
    )
```

profile of v0, /device:TPU:1, one launch (start us, length us, event | category | flops | bytes accessed | tf_op | source)
XLA Modules:
  0.0 788.0 jit_solution(4293421630822857458)
XLA Ops:
  10.9 12.6 %all-to-all-start = ((bf16[32,24,128]{2,1,0:T(8,128)(2,1)}), bf16[32,24,128]{2,1,0:T(8,128)(2,1)}, u32[]{:S(2)}, u32[]{:S(2)}) async-start(bf16[32,24,128]{2,1,0:T(8,128)(2,1)} %bitcast.14), calls=%async_computation | async-start | bytes 393216 | tf_op jit(solution)/shard_map/all_to_all | solution.py:110
  24.3 23.4 %all_gather.6 = bf16[24,4096]{1,0:T(8,128)(2,1)S(1)} all-gather(bf16[24,512]{1,0:T(8,128)(2,1)S(1)} %copy-done.30), channel_id=1, replica_groups=mesh['seq'=32,'dp'=8] {'dp'}, dimensions={1}, use_global_device_ids=true | all-gather | bytes 221184 | tf_op jit(solution)/shard_map/all_gather | solution.py:147
  47.8 22.9 %all_gather.7 = bf16[24,4096]{1,0:T(8,128)(2,1)S(1)} all-gather(bf16[24,512]{1,0:T(8,128)(2,1)S(1)} %copy-done.31), channel_id=1, replica_groups=mesh['seq'=32,'dp'=8] {'dp'}, dimensions={1}, use_global_device_ids=true | all-gather | bytes 221184 | tf_op jit(solution)/shard_map/all_gather | solution.py:148
  73.1 2.7 fusion.8
  76.0 1.8 convolution_bitcast_fusion.5
  78.7 1.5 fusion.56
  83.1 1.7 fusion.93
  84.8 1.7 convert_element_type.371
  86.5 5.4 copy.124
  92.4 24.4 %reduce = bf16[4096,24]{1,0:T(8,128)(2,1)} reduce(bf16[4096,1,24]{2,1,0:T(2,128)(2,1)} %bitcast.333, bf16[]{:T(256)} %broadcast.463), dimensions={1}, to_apply=%bitcast.319.reduce_sub_computation | reduce | bytes 393218
  116.8 3.3 reshape.412
  120.1 21.2 %all-to-all-start.1 = ((bf16[32,2,1536]{2,1,0:T(2,128)(2,1)}), bf16[32,2,1536]{2,1,0:T(2,128)(2,1)}, u32[]{:S(2)}, u32[]{:S(2)}) async-start(bf16[32,2,1536]{2,1,0:T(2,128)(2,1)} %reshape.412), calls=%async_computation.1 | async-start | bytes 393216 | tf_op jit(solution)/shard_map/all_to_all | solution.py:121
  141.3 1.7 copy.134
  143.0 10.2 %all-to-all-done.1 = bf16[32,2,1536]{2,1,0:T(2,128)(2,1)} async-done(((bf16[32,2,1536]{2,1,0:T(2,128)(2,1)}), bf16[32,2,1536]{2,1,0:T(2,128)(2,1)}, u32[]{:S(2)}, u32[]{:S(2)}) %all-to-all-start.1) | async-done | bytes 196640 | tf_op jit(solution)/shard_map/all_to_all | solution.py:121
  153.2 5.9 reshape.413
  159.0 5.1 copy.125
  166.2 1.9 copy.127
  168.1 2.9 fusion.109
  171.0 1.7 copy.128
  172.7 4.6 all-to-all-start.2
  177.3 1.7 copy.135
  179.0 10.2 %all-to-all-done.2 = bf16[32,24,128]{2,1,0:T(8,128)(2,1)} async-done(((bf16[32,24,128]{2,1,0:T(8,128)(2,1)}), bf16[32,24,128]{2,1,0:T(8,128)(2,1)}, u32[]{:S(2)}, u32[]{:S(2)}) %all-to-all-start.2) | async-done | bytes 196640 | tf_op jit(solution)/shard_map/all_to_all | solution.py:110
  189.2 4.8 all-to-all-start.4
  194.1 2.9 convolution_bitcast_fusion.4
  197.0 8.8 %all-to-all-done.4 = bf16[32,24,128]{2,1,0:T(8,128)(2,1)} async-done(((bf16[32,24,128]{2,1,0:T(8,128)(2,1)}), bf16[32,24,128]{2,1,0:T(8,128)(2,1)}, u32[]{:S(2)}, u32[]{:S(2)}) %all-to-all-start.4) | async-done | bytes 196640 | tf_op jit(solution)/shard_map/all_to_all | solution.py:110
  205.8 1.9 convolution_bitcast_fusion.3
  210.1 1.5 fusion.52
  211.6 1.7 multiply_add_fusion.2
  215.1 1.7 fusion.87
  216.8 1.7 convert_element_type.392
  218.5 4.9 copy.137
  223.4 24.6 %reduce.1 = bf16[4096,24]{1,0:T(8,128)(2,1)} reduce(bf16[4096,1,24]{2,1,0:T(2,128)(2,1)} %bitcast.336, bf16[]{:T(256)} %broadcast.463), dimensions={1}, to_apply=%bitcast.323.reduce_sub_computation | reduce | bytes 393218
  248.1 3.3 reshape.416
  251.4 16.4 %all_to_all.96 = bf16[32,2,1536]{2,1,0:T(2,128)(2,1)} all-to-all(bf16[32,2,1536]{2,1,0:T(2,128)(2,1)} %reshape.416), channel_id=1, replica_groups=mesh['seq'=32,'dp'=8] {'seq'}, dimensions={0} | all-to-all | bytes 393216 | tf_op jit(solution)/shard_map/all_to_all | solution.py:121
  267.8 5.9 reshape.417
  273.6 5.1 copy.138
  280.8 1.9 copy.140
  282.7 2.9 fusion.112
  285.6 1.7 copy.141
  287.3 4.5 all-to-all-start.6
  293.7 2.7 maximum_bitcast_fusion.21
  296.5 78.1 %all-reduce.1 = (f32[768]{0:T(1024)}, f32[768]{0:T(1024)}) all-reduce(f32[768]{0:T(1024)} %get-tuple-element.47, f32[768]{0:T(1024)} %get-tuple-element.44), channel_id=1, replica_groups=mesh['seq'=32,'dp'=8] {'seq','dp'}, use_global_device_ids=true, to_apply=%region_2.3 | all-reduce | flops 1536 | bytes 12288 | tf_op jit(solution)/shard_map/psum | solution.py:184
  374.6 1.7 convolution_bitcast_fusion.2
  380.2 2.3 multiply_add_fusion.5
  384.3 2.8 convolution_bitcast_fusion.1
  387.8 1.9 fusion.57
  390.5 40.9 %all-reduce.6 = bf16[2,24,4096]{2,0,1:T(2,128)(2,1)} all-reduce(f32[2,24,4096]{2,0,1:T(2,128)S(1)} %copy.147), channel_id=2, replica_groups=mesh['seq'=32,'dp'=8] {'dp'}, use_global_device_ids=true, to_apply=%region_5.6.clone | all-reduce | flops 196608 | bytes 1179648
  431.4 1.5 fusion.53
  434.4 1.7 multiply_subtract_fusion.4
  437.2 2.8 copy.143
  439.9 22.4 %reduce.3 = bf16[4096,24]{1,0:T(8,128)(2,1)S(1)} reduce(bf16[4096,1,24]{2,1,0:T(2,128)(2,1)S(1)} %bitcast.338, bf16[]{:T(256)} %broadcast.463), dimensions={1}, to_apply=%bitcast.325.reduce_sub_computation | reduce | bytes 393218
  462.4 2.1 reshape.418
  464.5 11.2 %all-to-all-start.7 = ((bf16[32,2,1536]{2,1,0:T(2,128)(2,1)}), bf16[32,2,1536]{2,1,0:T(2,128)(2,1)S(1)}, u32[]{:S(2)}, u32[]{:S(2)}) async-start(bf16[32,2,1536]{2,1,0:T(2,128)(2,1)} %reshape.418), calls=%async_computation.7 | async-start | bytes 393216 | tf_op jit(solution)/shard_map/all_to_all | solution.py:121
  476.8 2.8 copy.130
  479.6 22.4 %reduce.2 = bf16[4096,24]{1,0:T(8,128)(2,1)S(1)} reduce(bf16[4096,1,24]{2,1,0:T(2,128)(2,1)S(1)} %bitcast.334, bf16[]{:T(256)} %broadcast.463), dimensions={1}, to_apply=%bitcast.321.reduce_sub_computation | reduce | bytes 393218
  502.0 2.1 reshape.414
  504.9 9.8 %all-to-all-start.3 = ((bf16[32,2,1536]{2,1,0:T(2,128)(2,1)}), bf16[32,2,1536]{2,1,0:T(2,128)(2,1)S(1)}, u32[]{:S(2)}, u32[]{:S(2)}) async-start(bf16[32,2,1536]{2,1,0:T(2,128)(2,1)} %reshape.414), calls=%async_computation.3 | async-start | bytes 393216 | tf_op jit(solution)/shard_map/all_to_all | solution.py:121
  514.8 3.0 reshape.419
  517.7 2.1 copy.144
  520.8 5.7 all-to-all-done.3
  526.6 3.0 reshape.415
  529.5 2.1 copy.131
  537.0 241.8 %all-reduce.5.cloned.1.call-done = f32[64,2304]{1,0:T(8,128)} async-done(((f32[64,2304]{1,0:T(8,128)}), f32[64,2304]{1,0:T(8,128)}) %all-reduce.5.cloned.1.call-update) | async-done | bytes 589840 | tf_op jit(solution)/shard_map/psum | solution.py:184
  778.8 1.9 copy.209
  (130 shorter events, 38.5 us)
Async XLA Ops:
  7.2 1.0 copy-start
  7.2 17.2 %copy-start.30 = (bf16[24,512]{1,0:T(8,128)(2,1)S(1)}, bf16[24,512]{1,0:T(8,128)(2,1)}, u32[]{:S(2)}) copy-start(bf16[24,512]{1,0:T(8,128)(2,1)} %param.11) | copy-start | bytes 73732
  7.2 40.6 %copy-start.31 = (bf16[24,512]{1,0:T(8,128)(2,1)S(1)}, bf16[24,512]{1,0:T(8,128)(2,1)}, u32[]{:S(2)}) copy-start(bf16[24,512]{1,0:T(8,128)(2,1)} %param.12) | copy-start | bytes 73732
  9.3 0.8 copy-start.6
  10.9 65.1 %all-to-all-start = ((bf16[32,24,128]{2,1,0:T(8,128)(2,1)}), bf16[32,24,128]{2,1,0:T(8,128)(2,1)}, u32[]{:S(2)}, u32[]{:S(2)}) async-start(bf16[32,24,128]{2,1,0:T(8,128)(2,1)} %bitcast.14), calls=%async_computation | async-start | bytes 393216 | tf_op jit(solution)/shard_map/all_to_all | solution.py:110
  23.6 48.7 %copy-start.26 = (f32[1,64,32]{1,2,0:T(8,128)}, f32[1,64,32]{1,2,0:T(8,128)S(1)}, u32[]{:S(2)}) copy-start(f32[1,64,32]{1,2,0:T(8,128)S(1)} %get-tuple-element.101) | copy-start | bytes 24580
  73.0 2.7 copy-start.9
  73.1 2.7 copy-start.13
  77.8 0.9 copy-start.10
  77.8 1.0 copy-start.14
  80.2 1.2 copy-start.2
  120.1 33.1 %all-to-all-start.1 = ((bf16[32,2,1536]{2,1,0:T(2,128)(2,1)}), bf16[32,2,1536]{2,1,0:T(2,128)(2,1)}, u32[]{:S(2)}, u32[]{:S(2)}) async-start(bf16[32,2,1536]{2,1,0:T(2,128)(2,1)} %reshape.412), calls=%async_computation.1 | async-start | bytes 393216 | tf_op jit(solution)/shard_map/all_to_all | solution.py:121
  172.7 16.5 %all-to-all-start.2 = ((bf16[32,24,128]{2,1,0:T(8,128)(2,1)}), bf16[32,24,128]{2,1,0:T(8,128)(2,1)}, u32[]{:S(2)}, u32[]{:S(2)}) async-start(bf16[32,24,128]{2,1,0:T(8,128)(2,1)} %bitcast.352), calls=%async_computation.2 | async-start | bytes 393216 | tf_op jit(solution)/shard_map/all_to_all | solution.py:110
  189.2 16.6 %all-to-all-start.4 = ((bf16[32,24,128]{2,1,0:T(8,128)(2,1)}), bf16[32,24,128]{2,1,0:T(8,128)(2,1)}, u32[]{:S(2)}, u32[]{:S(2)}) async-start(bf16[32,24,128]{2,1,0:T(8,128)(2,1)} %bitcast.351), calls=%async_computation.4 | async-start | bytes 393216 | tf_op jit(solution)/shard_map/all_to_all | solution.py:110
  205.8 1.9 copy-start.8
  207.7 0.9 copy-start.11
  207.7 1.0 copy-start.15
  210.1 1.5 copy-start.4
  287.3 87.3 %all-to-all-start.6 = ((bf16[32,24,128]{2,1,0:T(8,128)(2,1)}), bf16[32,24,128]{2,1,0:T(8,128)(2,1)}, u32[]{:S(2)}, u32[]{:S(2)}) async-start(bf16[32,24,128]{2,1,0:T(8,128)(2,1)} %bitcast.350), calls=%async_computation.6 | async-start | bytes 393216 | tf_op jit(solution)/shard_map/all_to_all | solution.py:110
  376.3 0.9 copy-start.12
  376.3 1.0 copy-start.16
  377.3 1.4 copy-start.3
  378.7 1.4 copy-start.5
  382.5 1.4 copy-start.7
  389.9 41.6 %copy-start.21 = (f32[24,1,64,128]{3,2,1,0:T(8,128)S(1)}, f32[24,1,64,128]{3,2,1,0:T(8,128)}, u32[]{:S(2)}) copy-start(f32[24,1,64,128]{3,2,1,0:T(8,128)} %get-tuple-element.65) | copy-start | bytes 2359300
  389.9 41.6 %copy-start.22 = (f32[24,1,64,128]{3,2,1,0:T(8,128)S(1)}, f32[24,1,64,128]{3,2,1,0:T(8,128)}, u32[]{:S(2)}) copy-start(f32[24,1,64,128]{3,2,1,0:T(8,128)} %get-tuple-element.66) | copy-start | bytes 2359300
  431.4 1.5 copy-start.19
  431.4 1.5 copy-start.20
  462.4 13.3 %copy-start.17 = (f32[24,1,64,128]{3,2,1,0:T(8,128)S(1)}, f32[24,1,64,128]{3,2,1,0:T(8,128)}, u32[]{:S(2)}) copy-start(f32[24,1,64,128]{3,2,1,0:T(8,128)} %get-tuple-element.92) | copy-start | bytes 2359300
  462.4 13.3 %copy-start.18 = (f32[24,1,64,128]{3,2,1,0:T(8,128)S(1)}, f32[24,1,64,128]{3,2,1,0:T(8,128)}, u32[]{:S(2)}) copy-start(f32[24,1,64,128]{3,2,1,0:T(8,128)} %get-tuple-element.93) | copy-start | bytes 2359300
  464.5 40.4 %all-to-all-start.7 = ((bf16[32,2,1536]{2,1,0:T(2,128)(2,1)}), bf16[32,2,1536]{2,1,0:T(2,128)(2,1)S(1)}, u32[]{:S(2)}, u32[]{:S(2)}) async-start(bf16[32,2,1536]{2,1,0:T(2,128)(2,1)} %reshape.418), calls=%async_computation.7 | async-start | bytes 393216 | tf_op jit(solution)/shard_map/all_to_all | solution.py:121
  504.9 21.6 %all-to-all-start.3 = ((bf16[32,2,1536]{2,1,0:T(2,128)(2,1)}), bf16[32,2,1536]{2,1,0:T(2,128)(2,1)S(1)}, u32[]{:S(2)}, u32[]{:S(2)}) async-start(bf16[32,2,1536]{2,1,0:T(2,128)(2,1)} %reshape.414), calls=%async_computation.3 | async-start | bytes 393216 | tf_op jit(solution)/shard_map/all_to_all | solution.py:121
  514.7 264.1 %all-reduce.5.cloned.1.call-start = ((), (), s32[]{:S(2)}) async-start(), calls=%async_computation.8 | async-start | bytes 1179648 | tf_op jit(solution)/shard_map/psum | solution.py:184
  519.9 0.9 copy-start.23
  519.9 0.9 copy-start.28
  531.6 0.9 copy-start.24
  531.6 1.0 copy-start.25
  531.7 1.0 copy-start.32
  531.8 1.9 copy-start.27
  531.8 1.9 copy-start.29
  533.7 247.0 %copy-start.1 = (bf16[64,2304]{1,0:T(8,128)(2,1)S(1)}, bf16[64,2304]{1,0:T(8,128)(2,1)}, u32[]{:S(2)}) copy-start(bf16[64,2304]{1,0:T(8,128)(2,1)} %param.8) | copy-start | bytes 884740
Sparse Core Ops, SparseCore 0:
  534.9 243.8 all-reduce.4
where the time goes:
time: 800 us; the launch traced here: 788 us
  waiting for transfers between devices  277 us (35%)
  blocking collectives  182 us (23%)
  other arithmetic  116 us (14%)
  local copies, waits for them, and re-layouts  92.3 us (12%)
  starting transfers between devices  68.7 us (9%)
  matrix products  36.2 us (5%)
  between operations  15.9 us (2%)
    psum x1, waiting for transfers between devices, body(): lax.psum((weight_term, bias_one_term, bias_two_term), ('seq', 'dp'))  242 us
    unnamed x9, other arithmetic  95.9 us
    psum x1, blocking collectives, body(): lax.psum((weight_term, bias_one_term, bias_two_term), ('seq', 'dp'))  78.1 us
    unnamed x86, local copies, waits for them, and re-layouts  44.2 us
    all_to_all x3, starting transfers between devices, to_bins(): lax.all_to_all(block.reshape(1, block.shape[0], block.shape[1]), 'seq', s...  42.1 us
    unnamed x1, blocking collectives  40.9 us
    all_to_all x4, starting transfers between devices, to_columns(): lax.all_to_all(block.reshape(seq_count, group_width, block.shape[1]), 'se...  26.5 us
    all_gather x1, blocking collectives, body(): lax.all_gather(filter_one, 'dp', axis=1, tiled=True)  23.4 us
  transfers between devices with their start and end apart: 8, of which 5 were waited for; matrix products, arithmetic and copies ran while one was open for 7% of the time, Pallas kernels for 0%

commit v1 on v0

v1 whole, which is shorter than its diff:
```python
import functools
import math

import jax
import jax.numpy as jnp
import numpy as np
from jax import lax
from jax.experimental import pallas as pl
from jax.experimental.pallas import tpu as pltpu
from jax.sharding import PartitionSpec as P

SEQ = 32
DP = 8
ZN = 8
GROUP = 4
TILE = 128
EVENTS = 64
CH = 24
D = SEQ * CH
BINS = SEQ * TILE
COLS = 3 * CH
LANES = CH * TILE
f32 = jnp.float32
bf16 = jnp.bfloat16
MESH = pl.DeviceIdType.MESH
VMEM = pl.BlockSpec(memory_space=pltpu.VMEM)
SMEM = pl.BlockSpec(memory_space=pltpu.SMEM)
ANY = pl.BlockSpec(memory_space=pl.ANY)
LIMIT = 48 * 1024 * 1024


def tables():
    a = np.arange(SEQ)
    j = np.arange(TILE)
    k1 = np.arange(SEQ) + 0.25
    k2 = np.arange(TILE)
    first = np.exp(-2j * np.pi * np.outer(k1, a) / SEQ)
    turn = np.exp(-2j * np.pi * np.outer(k1, j) / BINS)
    second = np.exp(-2j * np.pi * np.outer(j, k2) / TILE)
    w1 = np.concatenate([first.real, first.imag], axis=0)
    w2 = np.block([[second.real, second.imag], [-second.imag, second.real]])
    inv2 = np.conj(second).T
    v2 = np.block([[inv2.real, inv2.imag], [-inv2.imag, inv2.real]])
    last = np.conj(first).T / BINS
    v1 = np.concatenate([last.real, -last.imag], axis=1)
    tw = np.stack([turn.real, turn.imag])

    def split(t):
        t = t.astype(np.float32)
        hi = t.astype(jnp.bfloat16)
        lo = (t - hi.astype(np.float32)).astype(jnp.bfloat16)
        return hi, lo

    w1h, w1l = split(w1)
    w2h, w2l = split(w2)
    v2h, v2l = split(v2)
    v1h, v1l = split(v1)
    return (
        np.concatenate([w1h, w1l], axis=1),
        np.concatenate([w2h, w2h, w2l], axis=0),
        np.concatenate([v2h, v2h, v2l], axis=0),
        np.concatenate([v1h, v1h, v1l], axis=1),
        tw.astype(np.float32),
    )


def dot(x, y):
    return jnp.dot(x, y, preferred_element_type=f32)


def split(x):
    hi = x.astype(bf16)
    lo = (x - hi.astype(f32)).astype(bf16)
    return hi, lo


def rnd(x):
    return x.astype(bf16).astype(f32)


def compute_kernel(
    lev_ref, wt_ref, b1_ref, b2_ref, cot_ref, f1_ref, f2_ref,
    w1_ref, w2_ref, v2_ref, v1_ref, tw_ref,
    out_ref, gf_ref, gw_ref,
    levs, rows, crows, val, g1, g2, hid, gm, m1, m2, gh,
    tmp, inv, hat1, hat2, hatv, hath, hatg, gpb,
):
    scale = 1.0 / math.sqrt(DP * BINS)
    base = lax.axis_index("seq") * CH

    def lanes(c):
        return slice(c * TILE, (c + 1) * TILE)

    def krows(c):
        return slice(c * SEQ, (c + 1) * SEQ)

    def put3(c, re, im):
        rh, rl = split(re)
        ih, il = split(im)
        tmp[krows(c), 0:128] = rh
        tmp[krows(c), 128:256] = ih
        tmp[krows(c), 256:384] = rl
        tmp[krows(c), 384:512] = il
        tmp[krows(c), 512:640] = rh
        tmp[krows(c), 640:768] = ih

    def forward(x_ref, dst):
        cr = tw_ref[0]
        ci = tw_ref[1]
        for p in range(CH // 2):
            x = x_ref[:, p * 256:(p + 1) * 256]
            part = dot(w1_ref[...], jnp.concatenate([x, x], axis=0))
            for h in range(2):
                re = part[0:32, lanes(h)]
                im = part[32:64, lanes(h)]
                put3(2 * p + h, re * cr - im * ci, re * ci + im * cr)
        dst[...] = dot(tmp[...], w2_ref[...])

    def inverse(left, right, conj, emit):
        cr = tw_ref[0]
        ci = tw_ref[1]
        for c in range(CH):
            lr = left[krows(c), 0:128]
            li = left[krows(c), 128:256]
            rr = right[krows(c), 0:128]
            ri = right[krows(c), 128:256]
            if conj:
                put3(c, lr * rr + li * ri, lr * ri - li * rr)
            else:
                put3(c, lr * rr - li * ri, lr * ri + li * rr)
        inv[...] = dot(tmp[...], v2_ref[...])
        for p in range(CH // 2):
            cols = []
            for h in range(2):
                c = 2 * p + h
                re = inv[krows(c), 0:128]
                im = inv[krows(c), 128:256]
                rh, rl = split(re * cr + im * ci)
                ih, il = split(im * cr - re * ci)
                cols.append(jnp.concatenate([rh, ih, rl, il, rh, ih], axis=0))
            res = dot(v1_ref[...], jnp.concatenate(cols, axis=1))
            for h in range(2):
                emit(2 * p + h, res[:, lanes(h)])

    for a in range(SEQ):
        levs[0:EVENTS, a * TILE:(a + 1) * TILE] = lev_ref[a % GROUP, a // GROUP]
    levs[EVENTS:, :] = jnp.zeros((TILE - EVENTS, BINS), bf16)
    for p in range(SEQ // 2):
        proj = dot(wt_ref[...], levs[0:EVENTS, p * 256:(p + 1) * 256])
        for h in range(2):
            a = 2 * p + h
            rows[a * COLS:(a + 1) * COLS, :] = proj[:, lanes(h)]
    for c in range(CH):
        val[:, lanes(c)] = rows[pl.ds(c, SEQ, stride=COLS), :].astype(bf16)
        g1[:, lanes(c)] = rows[pl.ds(CH + c, SEQ, stride=COLS), :].astype(bf16)
        g2[:, lanes(c)] = rows[pl.ds(2 * CH + c, SEQ, stride=COLS), :].astype(bf16)

    def load_filter(ref, dst):
        for d in range(DP):
            for q in range(BINS // DP // TILE):
                a = d * (BINS // DP // TILE) + q
                crows[a * CH:(a + 1) * CH, :] = ref[d, :, q * TILE:(q + 1) * TILE].astype(f32)
        for c in range(CH):
            hid[:, lanes(c)] = crows[pl.ds(c, SEQ, stride=CH), :].astype(bf16)
        forward(hid, dst)

    load_filter(f1_ref, hat1)
    load_filter(f2_ref, hat2)

    forward(val, hatv)

    def emit_one(c, conv):
        mixed = rnd(conv) + b1_ref[base + c] * val[:, lanes(c)].astype(f32)
        m1[:, lanes(c)] = mixed
        hid[:, lanes(c)] = (g1[:, lanes(c)].astype(f32) * mixed).astype(bf16)

    inverse(hat1, hatv, False, emit_one)
    forward(hid, hath)

    for a in range(SEQ):
        crows[a * CH:(a + 1) * CH, :] = cot_ref[a].astype(f32)

    def emit_two(c, conv):
        mixed = rnd(conv) + b2_ref[base + c] * hid[:, lanes(c)].astype(f32)
        up = crows[pl.ds(c, SEQ, stride=CH), :] * scale
        gate = g2[:, lanes(c)].astype(f32)
        rows[pl.ds(2 * CH + c, SEQ, stride=COLS), :] = up * mixed
        m2[:, lanes(c)] = gate * mixed
        gm[:, lanes(c)] = (up * gate).astype(bf16)

    inverse(hat2, hath, False, emit_two)
    for c in range(CH):
        crows[pl.ds(c, SEQ, stride=CH), :] = m2[:, lanes(c)]
    for a in range(SEQ):
        out_ref[a] = crows[a * CH:(a + 1) * CH, :].astype(bf16)

    forward(gm, hatg)
    bias_rows = []
    for c in range(CH):
        s = gm[:, lanes(c)].astype(f32) * hid[:, lanes(c)].astype(f32)
        bias_rows.append(jnp.sum(s, axis=0, keepdims=True))
    sum_two = jnp.sum(jnp.concatenate(bias_rows, axis=0), axis=1, keepdims=True)

    def emit_carried_two(c, conv):
        ghid = b2_ref[base + c] * gm[:, lanes(c)].astype(f32) + rnd(conv)
        gh[:, lanes(c)] = (ghid * g1[:, lanes(c)].astype(f32)).astype(bf16)
        rows[pl.ds(CH + c, SEQ, stride=COLS), :] = ghid * m1[:, lanes(c)]

    inverse(hat2, hatg, True, emit_carried_two)

    def emit_gf(which):
        def emit(c, conv):
            gf_ref[c // 3, which, :, (c % 3) * TILE:(c % 3 + 1) * TILE] = conv.astype(bf16)
        return emit

    inverse(hath, hatg, True, emit_gf(1))
    forward(gh, hatg)
    bias_rows = []
    for c in range(CH):
        s = gh[:, lanes(c)].astype(f32) * val[:, lanes(c)].astype(f32)
        bias_rows.append(jnp.sum(s, axis=0, keepdims=True))
    sum_one = jnp.sum(jnp.concatenate(bias_rows, axis=0), axis=1, keepdims=True)

    def emit_carried_one(c, conv):
        rows[pl.ds(c, SEQ, stride=COLS), :] = (
            b1_ref[base + c] * gh[:, lanes(c)].astype(f32) + rnd(conv)
        )

    inverse(hat1, hatg, True, emit_carried_one)
    inverse(hatv, hatg, True, emit_gf(0))
    for a in range(SEQ):
        gpb[:, a * TILE:(a + 1) * TILE] = rows[a * COLS:(a + 1) * COLS, :].astype(bf16)
    weight = lax.dot_general(
        gpb[...], levs[...], (((1,), (1,)), ((), ())), preferred_element_type=f32
    )
    sums = jnp.concatenate([sum_one, sum_two, jnp.zeros((CH, 1), f32)], axis=0)
    lane = lax.broadcasted_iota(jnp.int32, (COLS, TILE), 1)
    gw_ref[...] = weight + jnp.where(lane == EVENTS, sums, 0.0)


def compute(lev, wt, b1, b2, cot, f1, f2):
    w1, w2, v2, v1, tw = tables()
    return pl.pallas_call(
        compute_kernel,
        out_shape=(
            jax.ShapeDtypeStruct((SEQ, CH, TILE), bf16),
            jax.ShapeDtypeStruct((DP, 2, SEQ, 3 * TILE), bf16),
            jax.ShapeDtypeStruct((COLS, TILE), f32),
        ),
        in_specs=[VMEM, VMEM, SMEM, SMEM] + [VMEM] * 8,
        out_specs=(VMEM, VMEM, VMEM),
        scratch_shapes=[
            pltpu.VMEM((TILE, BINS), bf16),
            pltpu.VMEM((SEQ * COLS, TILE), f32),
            pltpu.VMEM((SEQ * CH, TILE), f32),
            pltpu.VMEM((SEQ, LANES), bf16),
            pltpu.VMEM((SEQ, LANES), bf16),
            pltpu.VMEM((SEQ, LANES), bf16),
            pltpu.VMEM((SEQ, LANES), bf16),
            pltpu.VMEM((SEQ, LANES), bf16),
            pltpu.VMEM((SEQ, LANES), f32),
            pltpu.VMEM((SEQ, LANES), f32),
            pltpu.VMEM((SEQ, LANES), bf16),
            pltpu.VMEM((SEQ * CH, 6 * TILE), bf16),
            pltpu.VMEM((SEQ * CH, 2 * TILE), f32),
            pltpu.VMEM((SEQ * CH, 2 * TILE), f32),
            pltpu.VMEM((SEQ * CH, 2 * TILE), f32),
            pltpu.VMEM((SEQ * CH, 2 * TILE), f32),
            pltpu.VMEM((SEQ * CH, 2 * TILE), f32),
            pltpu.VMEM((SEQ * CH, 2 * TILE), f32),
            pltpu.VMEM((COLS, BINS), bf16),
        ],
        compiler_params=pltpu.CompilerParams(vmem_limit_bytes=LIMIT),
        name="transforms",
    )(lev, wt, b1, b2, cot, f1, f2, w1, w2, v2, v1, tw)


def place():
    s = lax.axis_index("seq")
    d = lax.axis_index("dp")
    return s, d, s // GROUP, lax.rem(s, GROUP)


def seq_peer(s, i):
    return {"seq": lax.rem(s + i, SEQ)}


def dp_peer(d, i):
    return {"dp": lax.rem(d + i, DP)}


def z_peer(z, q, i):
    return {"seq": lax.rem(z + i, ZN) * GROUP + q}


def q_peer(z, q, r):
    return {"seq": z * GROUP + lax.rem(q + r, GROUP)}


def push(src, dst, send, recv, device):
    return pltpu.make_async_remote_copy(
        src_ref=src, dst_ref=dst, send_sem=send, recv_sem=recv,
        device_id=device, device_id_type=MESH,
    )


def greet(s, d):
    barrier = pltpu.get_barrier_semaphore()

    def hello_seq(i, _):
        pl.semaphore_signal(barrier, inc=1, device_id=seq_peer(s, i), device_id_type=MESH)
        return 0

    def hello_dp(i, _):
        pl.semaphore_signal(barrier, inc=1, device_id=dp_peer(d, i), device_id_type=MESH)
        return 0

    lax.fori_loop(1, SEQ, hello_seq, 0)
    lax.fori_loop(1, DP, hello_dp, 0)
    return lambda: pl.semaphore_wait(barrier, SEQ + DP - 2)


def each(low, high, f):
    def step(i, _):
        f(i)
        return 0

    lax.fori_loop(low, high, step, 0)


def entry_kernel(
    counts_ref, w_ref, cot_ref, f1_ref, f2_ref,
    lev_ref, wt_ref, cotg_ref, fg1_ref, fg2_ref,
    own, wtt, loc, zs, zr, gs, gr, fs, fr, cs, cr,
):
    s, d, z, q = place()
    wait_barrier = greet(s, d)
    levels = jnp.log1p(counts_ref[...].astype(f32)) - 3.0
    own[...] = levels.T.astype(bf16)
    wait_barrier()

    def z_copy(i):
        return push(own, lev_ref.at[q, z], zs.at[i], zr.at[i], z_peer(z, q, i))

    def g_copy(r, i):
        slot = lev_ref.at[q, lax.rem(z - i + ZN, ZN)]
        return push(slot, slot, gs.at[r, i], gr.at[r, i], q_peer(z, q, r))

    def f_copy(i, src, dst, k):
        return push(src, dst.at[d], fs.at[k, i], fr.at[k, i], dp_peer(d, i))

    def c_copy(i):
        return push(
            cot_ref.at[lax.rem(s + i, SEQ)], cotg_ref.at[s], cs.at[i], cr.at[i], seq_peer(s, i)
        )

    each(1, ZN, lambda i: z_copy(i).start())
    keep = pltpu.make_async_copy(own, lev_ref.at[q, z], loc.at[0])
    keep.start()
    keep_cot = pltpu.make_async_copy(cot_ref.at[s], cotg_ref.at[s], loc.at[1])
    keep_cot.start()
    keep_f1 = pltpu.make_async_copy(f1_ref, fg1_ref.at[d], loc.at[2])
    keep_f1.start()
    keep_f2 = pltpu.make_async_copy(f2_ref, fg2_ref.at[d], loc.at[3])
    keep_f2.start()

    def send_filters(i):
        f_copy(i, f1_ref, fg1_ref, 0).start()
        f_copy(i, f2_ref, fg2_ref, 1).start()

    each(1, DP, send_filters)
    each(1, SEQ, lambda i: c_copy(i).start())
    keep.wait()
    for r in range(1, GROUP):
        g_copy(r, 0).start()
    wtt[...] = w_ref[...].astype(f32).T
    for k in range(3):
        at = pl.multiple_of(k * D + s * CH, 8)
        wt_ref[k * CH:(k + 1) * CH, :] = wtt[pl.ds(at, CH), :].astype(bf16)

    def pass_on(i):
        z_copy(i).wait_recv()
        for r in range(1, GROUP):
            g_copy(r, i).start()

    each(1, ZN, pass_on)
    keep_cot.wait()
    keep_f1.wait()
    keep_f2.wait()
    each(1, ZN, lambda i: z_copy(i).wait_send())

    def end_filters(i):
        f_copy(i, f1_ref, fg1_ref, 0).wait()
        f_copy(i, f2_ref, fg2_ref, 1).wait()

    each(1, DP, end_filters)
    each(1, SEQ, lambda i: c_copy(i).wait())

    def end_group(i):
        for r in range(1, GROUP):
            g_copy(r, i).wait()

    each(0, ZN, end_group)


def entry(counts, w_in, cot, f1, f2):
    dma = pltpu.SemaphoreType.DMA
    return pl.pallas_call(
        entry_kernel,
        out_shape=(
            jax.ShapeDtypeStruct((GROUP, ZN, EVENTS, TILE), bf16),
            jax.ShapeDtypeStruct((COLS, EVENTS), bf16),
            jax.ShapeDtypeStruct((SEQ, CH, TILE), bf16),
            jax.ShapeDtypeStruct((DP, CH, BINS // DP), bf16),
            jax.ShapeDtypeStruct((DP, CH, BINS // DP), bf16),
        ),
        in_specs=[VMEM, VMEM, ANY, ANY, ANY],
        out_specs=(ANY, VMEM, ANY, ANY, ANY),
        scratch_shapes=[
            pltpu.VMEM((EVENTS, TILE), bf16),
            pltpu.VMEM((3 * D, EVENTS), f32),
            dma((4,)),
            dma((ZN,)),
            dma((ZN,)),
            dma((GROUP, ZN)),
            dma((GROUP, ZN)),
            dma((2, DP)),
            dma((2, DP)),
            dma((SEQ,)),
            dma((SEQ,)),
        ],
        compiler_params=pltpu.CompilerParams(
            collective_id=0, has_side_effects=True, vmem_limit_bytes=LIMIT
        ),
        name="entry",
    )(counts, w_in, cot, f1, f2)


def exit_kernel(
    out_ref, gf_ref, gw_ref,
    outg_ref, gf1_ref, gf2_ref, gwo_ref, gb_ref,
    gf_all, gw_in, gw_all, flat, loc, zs, zr, gs, gr, fs, fr, ws, wr, cs, cr,
):
    s, d, z, q = place()
    greet(s, d)()

    def w_copy(i):
        return push(gw_ref, gw_in.at[d], ws.at[i], wr.at[i], dp_peer(d, i))

    def f_copy(i):
        to = lax.rem(d + i, DP)
        return push(gf_ref.at[to], gf_all.at[d], fs.at[i], fr.at[i], dp_peer(d, i))

    def c_copy(i):
        return push(
            out_ref.at[lax.rem(s + i, SEQ)], outg_ref.at[s], cs.at[i], cr.at[i], seq_peer(s, i)
        )

    def z_copy(i):
        slot = gw_all.at[:, s]
        return push(slot, slot, zs.at[i], zr.at[i], z_peer(z, q, i))

    def g_copy(r, i):
        slot = gw_all.at[:, lax.rem(z - i + ZN, ZN) * GROUP + q]
        return push(slot, slot, gs.at[r, i], gr.at[r, i], q_peer(z, q, r))

    each(1, DP, lambda i: w_copy(i).start())
    keep_gw = pltpu.make_async_copy(gw_ref, gw_in.at[d], loc.at[0])
    keep_gw.start()
    each(1, DP, lambda i: f_copy(i).start())
    keep_gf = pltpu.make_async_copy(gf_ref.at[d], gf_all.at[d], loc.at[1])
    keep_gf.start()
    each(1, SEQ, lambda i: c_copy(i).start())
    keep_out = pltpu.make_async_copy(out_ref.at[s], outg_ref.at[s], loc.at[2])
    keep_out.start()
    keep_gw.wait()
    each(1, DP, lambda i: w_copy(i).wait())
    total = gw_in[0]
    for k in range(1, DP):
        total = total + gw_in[k]
    for k in range(3):
        gw_all[k, s] = total[k * CH:(k + 1) * CH]
    each(1, ZN, lambda i: z_copy(i).start())
    for r in range(1, GROUP):
        g_copy(r, 0).start()

    keep_gf.wait()
    each(1, DP, lambda i: f_copy(i).wait())

    def pass_on(i):
        z_copy(i).wait_recv()
        for r in range(1, GROUP):
            g_copy(r, i).start()

    each(1, ZN, pass_on)

    for which, dst in ((0, gf1_ref), (1, gf2_ref)):
        total = gf_all[0, which].astype(f32)
        for k in range(1, DP):
            total = total + gf_all[k, which].astype(f32)
        for c in range(3):
            for a in range(SEQ):
                flat[c:c + 1, a * TILE:(a + 1) * TILE] = total[
                    a:a + 1, c * TILE:(c + 1) * TILE
                ]
        dst[...] = flat[0:3, :].astype(bf16)

    each(1, ZN, lambda i: z_copy(i).wait_send())

    def end_group(i):
        for r in range(1, GROUP):
            g_copy(r, i).wait()

    each(0, ZN, end_group)
    for k in range(3):
        block = gw_all[k].reshape(D, TILE)
        for p in range(D // TILE):
            turned = block[p * TILE:(p + 1) * TILE, :].T
            at = k * D + p * TILE
            gwo_ref[:, at:at + TILE] = turned[0:EVENTS, :]
            if k < 2:
                gb_ref[k:k + 1, p * TILE:(p + 1) * TILE] = turned[EVENTS:EVENTS + 1, :]
    keep_out.wait()
    each(1, SEQ, lambda i: c_copy(i).wait())


def leave(out, gf, gw):
    dma = pltpu.SemaphoreType.DMA
    return pl.pallas_call(
        exit_kernel,
        out_shape=(
            jax.ShapeDtypeStruct((SEQ, CH, TILE), bf16),
            jax.ShapeDtypeStruct((3, BINS), bf16),
            jax.ShapeDtypeStruct((3, BINS), bf16),
            jax.ShapeDtypeStruct((EVENTS, 3 * D), f32),
            jax.ShapeDtypeStruct((2, D), f32),
        ),
        in_specs=[ANY, ANY, ANY],
        out_specs=(ANY, VMEM, VMEM, VMEM, VMEM),
        scratch_shapes=[
            pltpu.VMEM((DP, 2, SEQ, 3 * TILE), bf16),
            pltpu.VMEM((DP, COLS, TILE), f32),
            pltpu.VMEM((3, SEQ, CH, TILE), f32),
            pltpu.VMEM((8, BINS), f32),
            dma((3,)),
            dma((ZN,)),
            dma((ZN,)),
            dma((GROUP, ZN)),
            dma((GROUP, ZN)),
            dma((DP,)),
            dma((DP,)),
            dma((DP,)),
            dma((DP,)),
            dma((SEQ,)),
            dma((SEQ,)),
        ],
        compiler_params=pltpu.CompilerParams(
            collective_id=1, has_side_effects=True, vmem_limit_bytes=LIMIT
        ),
        name="leave",
    )(out, gf, gw)


def body(counts, w_in, bias_one, bias_two, filter_one, filter_two, cotangent):
    lev, wt, cot, f1, f2 = entry(
        counts[0], w_in, cotangent.reshape(SEQ, CH, TILE), filter_one, filter_two
    )
    out, gf, gw = compute(lev, wt, bias_one, bias_two, cot, f1, f2)
    out, gf1, gf2, gw, gb = leave(out, gf, gw)
    return out.reshape(1, D, TILE), gw, gb[0], gb[1], gf1, gf2


def solution(mesh):
    return jax.shard_map(
        body,
        mesh=mesh,
        in_specs=(
            P("dp", "seq", None),
            P(),
            P(),
            P(),
            P("seq", "dp"),
            P("seq", "dp"),
            P("dp", None, "seq"),
        ),
        out_specs=(
            P("dp", None, "seq"),
            P(),
            P(),
            P(),
            P(("seq", "dp"), None),
            P(("seq", "dp"), None),
        ),
        check_vma=False,
    )
```

time: 800 us -> 80.5 us (0.10); the launches traced: 788 us -> 80.2 us
  waiting for transfers between devices: 277 us -> 0 us
  blocking collectives: 182 us -> 0 us
  other arithmetic: 116 us -> 0 us
  local copies, waits for them, and re-layouts: 92.3 us -> 9.25 us
  Pallas kernels: 0 us -> 70.2 us
  starting transfers between devices: 68.7 us -> 0 us
  matrix products: 36.2 us -> 0 us
  between operations: 15.9 us -> 0.73 us
    psum x1 -> x0, waiting for transfers between devices: 242 us -> none  [body(): lax.psum((weight_term, bias_one_term, bias_two_term), ('seq', 'dp'))]
    unnamed x9 -> x0, other arithmetic: 95.9 us -> none
    psum x1 -> x0, blocking collectives: 78.1 us -> none  [body(): lax.psum((weight_term, bias_one_term, bias_two_term), ('seq', 'dp'))]
    pallas_call x0 -> x3, Pallas kernels: none -> 70.2 us  [the longest x1 32.9 us: leave(): pl.pallas_call(exit_kernel, out_shape=(jax.ShapeDtypeStruct((SEQ, CH, TIL...]
    all_to_all x7 -> x0, starting transfers between devices: 68.6 us -> none  [the longest x3 42.1 us: to_bins(): lax.all_to_all(block.reshape(1, block.shape[0], block.shape[1]), 'seq', s...]
    all_gather x2 -> x0, blocking collectives: 46.4 us -> none  [the longest x1 23.4 us: body(): lax.all_gather(filter_one, 'dp', axis=1, tiled=True)]
    unnamed x1 -> x0, blocking collectives: 40.9 us -> none
    dot_general x22 -> x0, matrix products: 36.2 us -> none  [the longest x5 9.73 us: transform(): jnp.einsum('rka,cab->crkb', first_table, blocks, precision=highest)]
  transfers between devices with their start and end apart: 8 -> 0, of which waited for: 5 -> 0; matrix products, arithmetic and copies ran while one was open for 7% -> 0% of each run, Pallas kernels for 0% -> 0%
where the time goes in v1:
time: 80.5 us; the launch traced here: 80.2 us
  Pallas kernels  70.2 us (87%)
  local copies, waits for them, and re-layouts  9.25 us (11%)
    pallas_call x1, Pallas kernels, leave(): pl.pallas_call(exit_kernel, out_shape=(jax.ShapeDtypeStruct((SEQ, CH, TIL...  32.9 us
    pallas_call x1, Pallas kernels, entry(): pl.pallas_call(entry_kernel, out_shape=(jax.ShapeDtypeStruct((GROUP, ZN,...  26 us
    pallas_call x1, Pallas kernels, compute(): pl.pallas_call(compute_kernel, out_shape=(jax.ShapeDtypeStruct((SEQ, CH,...  11.3 us
    unnamed x27, local copies, waits for them, and re-layouts  8.64 us

profile of v1, /device:TPU:1, one launch (start us, length us, event | category | flops | bytes accessed | tf_op | source)
XLA Modules:
  0.0 80.2 jit_solution(17442639382406548522)
XLA Ops:
  0.6 0.0 copy-start
  0.6 0.9 %copy.18 = s32[1,128,64]{2,1,0:T(8,128)S(1)} copy(s32[1,128,64]{1,2,0:T(8,128)} %param.12) | data formatting | bytes 65536 | tf_op args[0]
  1.5 0.0 copy-start.2
  1.6 1.0 %copy-done.2 = bf16[64,2304]{1,0:T(8,128)(2,1)S(1)} copy-done((bf16[64,2304]{1,0:T(8,128)(2,1)S(1)}, bf16[64,2304]{1,0:T(8,128)(2,1)}, u32[]{:S(2)}) %copy-start.2) | copy-done | bytes 294936
  2.5 0.0 copy-start.3
  2.5 0.9 %copy-done.3 = bf16[1,768,128]{2,1,0:T(8,128)(2,1)S(1)} copy-done((bf16[1,768,128]{2,1,0:T(8,128)(2,1)S(1)}, bf16[1,768,128]{2,1,0:T(8,128)(2,1)}, u32[]{:S(2)}) %copy-start.3) | copy-done | bytes 196632
  3.4 0.0 copy-start.5
  3.4 0.7 copy-done.5
  4.2 0.0 copy-start.6
  4.2 0.7 copy-done.6
  4.9 0.0 copy-start.4
  4.9 0.0 copy-start.7
  4.9 0.0 copy-start.8
  4.9 26.0 %entry.1 = (bf16[4,8,64,128]{3,2,1,0:T(8,128)(2,1)S(1)}, bf16[72,64]{1,0:T(8,128)(2,1)S(1)}, bf16[32,24,128]{2,1,0:T(8,128)(2,1)S(1)}, bf16[8,24,512]{2,1,0:T(8,128)(2,1)S(1)}, bf16[8,24,512]{2,1,0:T(8,128)(2,1)S(1)}) custom-call(s32[128,64]{1,0:T(8,128)S(1)} %bitcast.3, bf16[64,2304]{1,0:T(8,128)(2,1)S(1)} %copy-done.2, bf16[32,24,128]{2,1,0:T(8,128)(2,1)S(1)} %bitcast.5, ...), custom_call_target="tpu_custom_call" | custom-call | tf_op jit(solution)/shard_map/entry/pallas_call | solution.py:408
  30.9 0.0 copy-start.10
  30.9 0.0 copy-start.9
  30.9 0.0 copy-done
  30.9 0.0 copy-done.4
  31.0 0.0 copy-done.7
  31.0 0.0 copy-done.8
  31.0 0.6 copy-done.10
  31.6 0.0 copy-done.9
  31.6 0.0 copy-start.1
  31.6 1.0 %copy-done.1 = bf16[768,256]{1,0:T(8,128)(2,1)S(1)} copy-done((bf16[768,256]{1,0:T(8,128)(2,1)S(1)}, bf16[768,256]{1,0:T(8,128)(2,1)}, u32[]{:S(2)}) %copy-start.1) | copy-done | bytes 393240
  32.6 11.3 %transforms.1 = (bf16[32,24,128]{2,1,0:T(8,128)(2,1)S(1)}, bf16[8,2,32,384]{3,2,1,0:T(8,128)(2,1)S(1)}, f32[72,128]{1,0:T(8,128)S(1)}) custom-call(bf16[4,8,64,128]{3,2,1,0:T(8,128)(2,1)S(1)} %get-tuple-element.19.lev_ref, bf16[72,64]{1,0:T(8,128)(2,1)S(1)} %get-tuple-element.20.wt_ref, f32[768]{0:T(1024)S(1)} %copy-done.9, f32[768]{0:T(1024)S(1)} %copy-done.10, ...), custom_call_target="tpu_custom_call" | custom-call | tf_op jit(solution)/shard_map/transforms/pallas_call | solution.py:243
  43.9 32.9 %leave.1 = (bf16[32,24,128]{2,1,0:T(8,128)(2,1)S(1)}, bf16[3,4096]{1,0:T(4,128)(2,1)S(1)}, bf16[3,4096]{1,0:T(4,128)(2,1)S(1)}, f32[64,2304]{1,0:T(8,128)S(1)}, f32[2,768]{1,0:T(2,128)S(1)}) custom-call(bf16[32,24,128]{2,1,0:T(8,128)(2,1)S(1)} %get-tuple-element.24.out_ref, bf16[8,2,32,384]{3,2,1,0:T(8,128)(2,1)S(1)} %get-tuple-element.25.gf_ref, ...), custom_call_target="tpu_custom_call" | custom-call | tf_op jit(solution)/shard_map/leave/pallas_call | solution.py:529
  76.8 0.6 slice_reduce_fusion
  77.5 0.7 copy.23
  78.1 0.8 %copy.24 = f32[64,2304]{1,0:T(8,128)} copy(f32[64,2304]{1,0:T(8,128)S(1)} %get-tuple-element.41) | data formatting | bytes 1179648
  79.0 0.6 copy.25
  79.6 0.6 copy.26
Async XLA Ops:
  0.6 30.3 %copy-start = (bf16[768,256]{1,0:T(8,128)(2,1)S(1)}, bf16[768,256]{1,0:T(8,128)(2,1)}, u32[]{:S(2)}) copy-start(bf16[768,256]{1,0:T(8,128)(2,1)} %constant.12.clone.v2_ref) | copy-start | bytes 1179652
  1.5 1.0 %copy-start.2 = (bf16[64,2304]{1,0:T(8,128)(2,1)S(1)}, bf16[64,2304]{1,0:T(8,128)(2,1)}, u32[]{:S(2)}) copy-start(bf16[64,2304]{1,0:T(8,128)(2,1)} %w_ref.1) | copy-start | bytes 884740
  2.5 0.9 %copy-start.3 = (bf16[1,768,128]{2,1,0:T(8,128)(2,1)S(1)}, bf16[1,768,128]{2,1,0:T(8,128)(2,1)}, u32[]{:S(2)}) copy-start(bf16[1,768,128]{2,1,0:T(8,128)(2,1)} %param.18) | copy-start | bytes 589828
  3.4 0.7 copy-start.5
  4.2 0.7 copy-start.6
  4.9 26.0 %copy-start.4 = (f32[2,32,128]{2,1,0:T(8,128)S(1)}, f32[2,32,128]{2,1,0:T(8,128)}, u32[]{:S(2)}) copy-start(f32[2,32,128]{2,1,0:T(8,128)} %constant.14.clone.tw_ref) | copy-start | bytes 98308
  4.9 26.0 %copy-start.7 = (bf16[32,192]{1,0:T(8,128)(2,1)S(1)}, bf16[32,192]{1,0:T(8,128)(2,1)}, u32[]{:S(2)}) copy-start(bf16[32,192]{1,0:T(8,128)(2,1)} %constant.13.clone.v1_ref) | copy-start | bytes 36868
  4.9 26.0 %copy-start.8 = (bf16[64,64]{1,0:T(8,128)(2,1)S(1)}, bf16[64,64]{1,0:T(8,128)(2,1)}, u32[]{:S(2)}) copy-start(bf16[64,64]{1,0:T(8,128)(2,1)} %constant.10.clone.w1_ref) | copy-start | bytes 24580
  30.9 0.7 copy-start.10
  30.9 0.7 copy-start.9
  31.6 1.0 %copy-start.1 = (bf16[768,256]{1,0:T(8,128)(2,1)S(1)}, bf16[768,256]{1,0:T(8,128)(2,1)}, u32[]{:S(2)}) copy-start(bf16[768,256]{1,0:T(8,128)(2,1)} %constant.11.clone.w2_ref) | copy-start | bytes 1179652

commit v2 on v0

v2 whole, which is shorter than its diff:
```python
import functools
import math

import jax
import jax.numpy as jnp
import numpy as np
from jax import lax
from jax.experimental import pallas as pl
from jax.experimental.pallas import tpu as pltpu
from jax.sharding import PartitionSpec as P

SEQ = 32
DP = 8
ZN = 8
GROUP = 4
TILE = 128
EVENTS = 64
CH = 24
D = SEQ * CH
BINS = SEQ * TILE
COLS = 3 * CH
LANES = CH * TILE
f32 = jnp.float32
bf16 = jnp.bfloat16
MESH = pl.DeviceIdType.MESH
VMEM = pl.BlockSpec(memory_space=pltpu.VMEM)
SMEM = pl.BlockSpec(memory_space=pltpu.SMEM)
ANY = pl.BlockSpec(memory_space=pl.ANY)
LIMIT = 56 * 1024 * 1024


def tables():
    a = np.arange(SEQ)
    j = np.arange(TILE)
    k1 = np.arange(SEQ) + 0.25
    k2 = np.arange(TILE)
    first = np.exp(-2j * np.pi * np.outer(k1, a) / SEQ)
    turn = np.exp(-2j * np.pi * np.outer(k1, j) / BINS)
    second = np.exp(-2j * np.pi * np.outer(j, k2) / TILE)
    w1 = np.concatenate([first.real, first.imag], axis=0)
    w2 = np.block([[second.real, second.imag], [-second.imag, second.real]])
    inv2 = np.conj(second).T
    v2 = np.block([[inv2.real, inv2.imag], [-inv2.imag, inv2.real]])
    last = np.conj(first).T / BINS
    v1 = np.concatenate([last.real, -last.imag], axis=1)

    table = np.zeros((640, 2 * TILE), np.float32)
    table[0:256] = w2
    table[256:512] = v2
    table[512:576, 0:32] = w1
    table[576:608, 0:64] = v1
    table[608:640, 0:128] = turn.real
    table[608:640, 128:256] = turn.imag
    return table


def dot(x, y):
    return jnp.dot(x, y, preferred_element_type=f32)


def split(x):
    hi = x.astype(bf16)
    lo = (x - hi.astype(f32)).astype(bf16)
    return hi, lo


def rnd(x):
    return x.astype(bf16).astype(f32)


def place():
    s = lax.axis_index("seq")
    d = lax.axis_index("dp")
    return s, d, s // GROUP, lax.rem(s, GROUP)


def seq_peer(s, i):
    return {"seq": lax.rem(s + i, SEQ)}


def dp_peer(d, i):
    return {"dp": lax.rem(d + i, DP)}


def z_peer(z, q, i):
    return {"seq": lax.rem(z + i, ZN) * GROUP + q}


def q_peer(z, q, r):
    return {"seq": z * GROUP + lax.rem(q + r, GROUP)}


def push(src, dst, send, recv, device):
    return pltpu.make_async_remote_copy(
        src_ref=src, dst_ref=dst, send_sem=send, recv_sem=recv,
        device_id=device, device_id_type=MESH,
    )


def greet(s, d):
    barrier = pltpu.get_barrier_semaphore()

    def hello_seq(i, _):
        pl.semaphore_signal(barrier, inc=1, device_id=seq_peer(s, i), device_id_type=MESH)
        return 0

    def hello_dp(i, _):
        pl.semaphore_signal(barrier, inc=1, device_id=dp_peer(d, i), device_id_type=MESH)
        return 0

    lax.fori_loop(1, SEQ, hello_seq, 0)
    lax.fori_loop(1, DP, hello_dp, 0)
    return lambda: pl.semaphore_wait(barrier, SEQ + DP - 2)


def each(low, high, f):
    def step(i, _):
        f(i)
        return 0

    lax.fori_loop(low, high, step, 0)


def whole_kernel(
    counts_in, w_in, b1_ref, b2_ref, cot_in, f1_in, f2_in,
    table_in,
    outg_ref, gf1_ref, gf2_ref, gwo_ref, gb_ref,
    counts_ref, w_ref, table, w1_ref, w2_ref, v2_ref, v1_ref, tw_ref,
    own, wtt, wt_ref, lev_ref, cot_ref, f1_ref, f2_ref,
    levs, rows, crows, val, g1, g2, hid, gm, m1, m2, gh,
    tmp, inv, hat1, hat2, hatv, hath, hatg, gpb,
    out_s, gf_s, gwp, gf_all, gw_in, gw_all, flat,
    pre, loc, zs, zr, gs, gr, fs, fr, cs, cr,
    os_, or_, hs, hr, ks, kr, azs, azr, ags, agr, vs, vr,
):
    s, d, z, q = place()
    wait_barrier = greet(s, d)
    loads = [
        pltpu.make_async_copy(a, b, pre.at[i])
        for i, (a, b) in enumerate((
            (counts_in, counts_ref), (w_in, w_ref), (table_in, table),
        ))
    ]
    for load in loads:
        load.start()
    scale = 1.0 / math.sqrt(DP * BINS)
    base = s * CH

    def lanes(c):
        return slice(c * TILE, (c + 1) * TILE)

    def krows(c):
        return slice(c * SEQ, (c + 1) * SEQ)

    def put3(c, re, im):
        rh, rl = split(re)
        ih, il = split(im)
        tmp[krows(c), 0:128] = rh
        tmp[krows(c), 128:256] = ih
        tmp[krows(c), 256:384] = rl
        tmp[krows(c), 384:512] = il
        tmp[krows(c), 512:640] = rh
        tmp[krows(c), 640:768] = ih

    def forward(x_ref, dst):
        cr_ = tw_ref[0]
        ci_ = tw_ref[1]
        for p in range(CH // 2):
            x = x_ref[:, p * 256:(p + 1) * 256]
            part = dot(w1_ref[...], jnp.concatenate([x, x], axis=0))
            for h in range(2):
                re = part[0:32, lanes(h)]
                im = part[32:64, lanes(h)]
                put3(2 * p + h, re * cr_ - im * ci_, re * ci_ + im * cr_)
        dst[...] = dot(tmp[...], w2_ref[...])

    def inverse(left, right, conj, emit):
        cr_ = tw_ref[0]
        ci_ = tw_ref[1]
        for c in range(CH):
            lr = left[krows(c), 0:128]
            li = left[krows(c), 128:256]
            rr = right[krows(c), 0:128]
            ri = right[krows(c), 128:256]
            if conj:
                put3(c, lr * rr + li * ri, lr * ri - li * rr)
            else:
                put3(c, lr * rr - li * ri, lr * ri + li * rr)
        inv[...] = dot(tmp[...], v2_ref[...])
        for p in range(CH // 2):
            cols = []
            for h in range(2):
                c = 2 * p + h
                re = inv[krows(c), 0:128]
                im = inv[krows(c), 128:256]
                rh, rl = split(re * cr_ + im * ci_)
                ih, il = split(im * cr_ - re * ci_)
                cols.append(jnp.concatenate([rh, ih, rl, il, rh, ih], axis=0))
            res = dot(v1_ref[...], jnp.concatenate(cols, axis=1))
            for h in range(2):
                emit(2 * p + h, res[:, lanes(h)])

    def z_copy(i):
        return push(own, lev_ref.at[q, z], zs.at[i], zr.at[i], z_peer(z, q, i))

    def g_copy(r, i):
        slot = lev_ref.at[q, lax.rem(z - i + ZN, ZN)]
        return push(slot, slot, gs.at[r, i], gr.at[r, i], q_peer(z, q, r))

    def f_copy(i, src, dst, k):
        return push(src, dst.at[d], fs.at[k, i], fr.at[k, i], dp_peer(d, i))

    def c_copy(i):
        return push(
            cot_in.at[lax.rem(s + i, SEQ)], cot_ref.at[s], cs.at[i], cr.at[i], seq_peer(s, i)
        )

    def o_copy(i):
        return push(
            out_s.at[lax.rem(s + i, SEQ)], outg_ref.at[s], os_.at[i], or_.at[i], seq_peer(s, i)
        )

    def h_copy(which, i):
        to = lax.rem(d + i, DP)
        return push(
            gf_s.at[which, to], gf_all.at[which, d], hs.at[which, i], hr.at[which, i],
            dp_peer(d, i),
        )

    def k_copy(part, i):
        at = slice(0, CH) if part == 0 else slice(CH, COLS)
        return push(
            gwp.at[at], gw_in.at[d, at], ks.at[part, i], kr.at[part, i], dp_peer(d, i)
        )

    def az_copy(i):
        slot = gw_all.at[1:3, s]
        return push(slot, slot, azs.at[i], azr.at[i], z_peer(z, q, i))

    def ag_copy(r, i):
        slot = gw_all.at[1:3, lax.rem(z - i + ZN, ZN) * GROUP + q]
        return push(slot, slot, ags.at[r, i], agr.at[r, i], q_peer(z, q, r))

    def v_copy(i):
        slot = gw_all.at[0, s]
        return push(slot, slot, vs.at[i], vr.at[i], seq_peer(s, i))

    loads[0].wait()
    levels = jnp.log1p(counts_ref[...].astype(f32)) - 3.0
    own[...] = levels.astype(bf16)
    lev_ref[q, z] = own[...]
    wait_barrier()
    each(1, ZN, lambda i: z_copy(i).start())

    def send_filters(i):
        f_copy(i, f1_in, f1_ref, 0).start()
        f_copy(i, f2_in, f2_ref, 1).start()

    each(1, DP, send_filters)
    for r in range(1, GROUP):
        g_copy(r, 0).start()
    each(1, SEQ, lambda i: c_copy(i).start())
    keeps = [
        pltpu.make_async_copy(f1_in, f1_ref.at[d], loc.at[0]),
        pltpu.make_async_copy(f2_in, f2_ref.at[d], loc.at[1]),
        pltpu.make_async_copy(cot_in.at[s], cot_ref.at[s], loc.at[2]),
    ]
    for keep in keeps:
        keep.start()
    loads[1].wait()
    wtt[...] = w_ref[...].astype(f32).T
    for k in range(3):
        at = pl.multiple_of(k * D + s * CH, 8)
        wt_ref[k * CH:(k + 1) * CH, :] = wtt[pl.ds(at, CH), :].astype(bf16)
    levs[EVENTS:, :] = jnp.zeros((TILE - EVENTS, BINS), bf16)
    loads[2].wait()
    for at, ref in ((0, w2_ref), (256, v2_ref)):
        hi, lo = split(table[at:at + 256, :])
        ref[0:256, :] = hi
        ref[256:512, :] = hi
        ref[512:768, :] = lo
    hi, lo = split(table[512:576, 0:32])
    w1_ref[...] = jnp.concatenate([hi, lo], axis=1)
    hi, lo = split(table[576:608, 0:64])
    v1_ref[...] = jnp.concatenate([hi, hi, lo], axis=1)
    tw_ref[0] = table[608:640, 0:128]
    tw_ref[1] = table[608:640, 128:256]

    def pass_on(i):
        z_copy(i).wait_recv()
        for r in range(1, GROUP):
            g_copy(r, i).start()

    each(1, ZN, pass_on)

    def load_filter(ref, dst):
        for e in range(DP):
            for p in range(BINS // DP // TILE):
                a = e * (BINS // DP // TILE) + p
                crows[a * CH:(a + 1) * CH, :] = ref[e, :, p * TILE:(p + 1) * TILE].astype(f32)
        for c in range(CH):
            hid[:, lanes(c)] = crows[pl.ds(c, SEQ, stride=CH), :].astype(bf16)
        forward(hid, dst)

    keeps[0].wait()
    each(1, DP, lambda i: f_copy(i, f1_in, f1_ref, 0).wait())
    load_filter(f1_ref, hat1)
    keeps[1].wait()
    each(1, DP, lambda i: f_copy(i, f2_in, f2_ref, 1).wait())
    load_filter(f2_ref, hat2)

    each(1, ZN, lambda i: z_copy(i).wait_send())

    def end_group(i):
        for r in range(1, GROUP):
            g_copy(r, i).wait()

    each(0, ZN, end_group)
    for a in range(SEQ):
        levs[0:EVENTS, a * TILE:(a + 1) * TILE] = lev_ref[a % GROUP, a // GROUP]
    for p in range(SEQ // 2):
        proj = dot(wt_ref[...], levs[0:EVENTS, p * 256:(p + 1) * 256])
        for h in range(2):
            a = 2 * p + h
            rows[a * COLS:(a + 1) * COLS, :] = proj[:, lanes(h)]
    for c in range(CH):
        val[:, lanes(c)] = rows[pl.ds(c, SEQ, stride=COLS), :].astype(bf16)
        g1[:, lanes(c)] = rows[pl.ds(CH + c, SEQ, stride=COLS), :].astype(bf16)
        g2[:, lanes(c)] = rows[pl.ds(2 * CH + c, SEQ, stride=COLS), :].astype(bf16)
    forward(val, hatv)

    def emit_one(c, conv):
        mixed = rnd(conv) + b1_ref[base + c] * val[:, lanes(c)].astype(f32)
        m1[:, lanes(c)] = mixed
        hid[:, lanes(c)] = (g1[:, lanes(c)].astype(f32) * mixed).astype(bf16)

    inverse(hat1, hatv, False, emit_one)
    forward(hid, hath)

    keeps[2].wait()
    each(1, SEQ, lambda i: c_copy(i).wait())
    for a in range(SEQ):
        crows[a * CH:(a + 1) * CH, :] = cot_ref[a].astype(f32)

    def emit_two(c, conv):
        mixed = rnd(conv) + b2_ref[base + c] * hid[:, lanes(c)].astype(f32)
        up = crows[pl.ds(c, SEQ, stride=CH), :] * scale
        gate = g2[:, lanes(c)].astype(f32)
        rows[pl.ds(2 * CH + c, SEQ, stride=COLS), :] = up * mixed
        m2[:, lanes(c)] = gate * mixed
        gm[:, lanes(c)] = (up * gate).astype(bf16)

    inverse(hat2, hath, False, emit_two)
    for c in range(CH):
        crows[pl.ds(c, SEQ, stride=CH), :] = m2[:, lanes(c)]
    for a in range(SEQ):
        out_s[a] = crows[a * CH:(a + 1) * CH, :].astype(bf16)
    each(1, SEQ, lambda i: o_copy(i).start())
    keep_out = pltpu.make_async_copy(out_s.at[s], outg_ref.at[s], loc.at[3])
    keep_out.start()

    def bias_sums(x_ref, y_ref):
        parts = []
        for c in range(CH):
            t = x_ref[:, lanes(c)].astype(f32) * y_ref[:, lanes(c)].astype(f32)
            parts.append(jnp.sum(t, axis=0, keepdims=True))
        return jnp.sum(jnp.concatenate(parts, axis=0), axis=1, keepdims=True)

    def weight_rows(low, high, sums):
        for a in range(SEQ):
            gpb[low:high, a * TILE:(a + 1) * TILE] = rows[
                a * COLS + low:a * COLS + high, :
            ].astype(bf16)
        weight = lax.dot_general(
            gpb[low:high, :], levs[...], (((1,), (1,)), ((), ())), preferred_element_type=f32
        )
        lane = lax.broadcasted_iota(jnp.int32, (high - low, TILE), 1)
        gwp[low:high, :] = weight + jnp.where(lane == EVENTS, sums, 0.0)
        gw_in[d, low:high, :] = gwp[low:high, :]

    def total_rows(low, high):
        total = gw_in[0, low:high, :]
        for k in range(1, DP):
            total = total + gw_in[k, low:high, :]
        for k in range(low // CH, high // CH):
            gw_all[k, s] = total[k * CH - low:(k + 1) * CH - low].astype(bf16)

    def emit_gf(which):
        def emit(c, conv):
            gf_s[which, c // 3, :, (c % 3) * TILE:(c % 3 + 1) * TILE] = conv.astype(bf16)
        return emit

    def finish_filter(which, dst):
        each(1, DP, lambda i: h_copy(which, i).wait())
        total = gf_all[which, 0].astype(f32)
        for k in range(1, DP):
            total = total + gf_all[which, k].astype(f32)
        for c in range(3):
            for a in range(SEQ):
                flat[c:c + 1, a * TILE:(a + 1) * TILE] = total[a:a + 1, lanes(c)]
        dst[...] = flat[0:3, :].astype(bf16)

    forward(gm, hatg)
    sum_two = bias_sums(gm, hid)

    def emit_carried_two(c, conv):
        ghid = b2_ref[base + c] * gm[:, lanes(c)].astype(f32) + rnd(conv)
        gh[:, lanes(c)] = (ghid * g1[:, lanes(c)].astype(f32)).astype(bf16)
        rows[pl.ds(CH + c, SEQ, stride=COLS), :] = ghid * m1[:, lanes(c)]

    inverse(hat2, hatg, True, emit_carried_two)
    weight_rows(CH, COLS, jnp.concatenate([sum_two, jnp.zeros((CH, 1), f32)], axis=0))
    each(1, DP, lambda i: k_copy(1, i).start())

    inverse(hath, hatg, True, emit_gf(1))
    gf_all[1, d] = gf_s[1, d]
    each(1, DP, lambda i: h_copy(1, i).start())

    forward(gh, hatg)
    sum_one = bias_sums(gh, val)

    def emit_carried_one(c, conv):
        rows[pl.ds(c, SEQ, stride=COLS), :] = (
            b1_ref[base + c] * gh[:, lanes(c)].astype(f32) + rnd(conv)
        )

    inverse(hat1, hatg, True, emit_carried_one)
    weight_rows(0, CH, sum_one)
    each(1, DP, lambda i: k_copy(0, i).start())

    each(1, DP, lambda i: k_copy(1, i).wait())
    total_rows(CH, COLS)
    each(1, ZN, lambda i: az_copy(i).start())
    for r in range(1, GROUP):
        ag_copy(r, 0).start()

    inverse(hatv, hatg, True, emit_gf(0))
    gf_all[0, d] = gf_s[0, d]
    each(1, DP, lambda i: h_copy(0, i).start())

    each(1, DP, lambda i: k_copy(0, i).wait())
    total_rows(0, CH)
    each(1, SEQ, lambda i: v_copy(i).start())

    def pass_on_weights(i):
        az_copy(i).wait_recv()
        for r in range(1, GROUP):
            ag_copy(r, i).start()

    each(1, ZN, pass_on_weights)
    finish_filter(1, gf2_ref)
    finish_filter(0, gf1_ref)
    each(1, ZN, lambda i: az_copy(i).wait_send())

    def end_weights(i):
        for r in range(1, GROUP):
            ag_copy(r, i).wait()

    def turn(k):
        block = gw_all[k].astype(f32).reshape(D, TILE)
        for p in range(D // TILE):
            turned = block[p * TILE:(p + 1) * TILE, :].T
            at = k * D + p * TILE
            gwo_ref[:, at:at + TILE] = turned[0:EVENTS, :]
            if k < 2:
                gb_ref[k:k + 1, p * TILE:(p + 1) * TILE] = turned[EVENTS:EVENTS + 1, :]

    each(0, ZN, end_weights)
    turn(1)
    turn(2)
    each(1, SEQ, lambda i: v_copy(i).wait())
    turn(0)
    keep_out.wait()
    each(1, SEQ, lambda i: o_copy(i).wait())


def whole(counts, w_in, b1, b2, cot, f1, f2):
    dma = pltpu.SemaphoreType.DMA
    vm = pltpu.VMEM
    spec = (SEQ * CH, 2 * TILE)
    return pl.pallas_call(
        whole_kernel,
        out_shape=(
            jax.ShapeDtypeStruct((SEQ, CH, TILE), bf16),
            jax.ShapeDtypeStruct((3, BINS), bf16),
            jax.ShapeDtypeStruct((3, BINS), bf16),
            jax.ShapeDtypeStruct((EVENTS, 3 * D), f32),
            jax.ShapeDtypeStruct((2, D), f32),
        ),
        in_specs=[ANY, ANY, SMEM, SMEM] + [ANY] * 4,
        out_specs=(ANY, VMEM, VMEM, VMEM, VMEM),
        scratch_shapes=[
            vm((EVENTS, TILE), jnp.int32),
            vm((EVENTS, 3 * D), bf16),
            vm((640, 2 * TILE), f32),
            vm((2 * SEQ, 2 * SEQ), bf16),
            vm((6 * TILE, 2 * TILE), bf16),
            vm((6 * TILE, 2 * TILE), bf16),
            vm((SEQ, 6 * SEQ), bf16),
            vm((2, SEQ, TILE), f32),
            vm((EVENTS, TILE), bf16),
            vm((3 * D, EVENTS), f32),
            vm((COLS, EVENTS), bf16),
            vm((GROUP, ZN, EVENTS, TILE), bf16),
            vm((SEQ, CH, TILE), bf16),
            vm((DP, CH, BINS // DP), bf16),
            vm((DP, CH, BINS // DP), bf16),
            vm((TILE, BINS), bf16),
            vm((SEQ * COLS, TILE), f32),
            vm((SEQ * CH, TILE), f32),
            vm((SEQ, LANES), bf16),
            vm((SEQ, LANES), bf16),
            vm((SEQ, LANES), bf16),
            vm((SEQ, LANES), bf16),
            vm((SEQ, LANES), bf16),
            vm((SEQ, LANES), f32),
            vm((SEQ, LANES), f32),
            vm((SEQ, LANES), bf16),
            vm((SEQ * CH, 6 * TILE), bf16),
            vm(spec, f32),
            vm(spec, f32),
            vm(spec, f32),
            vm(spec, f32),
            vm(spec, f32),
            vm(spec, f32),
            vm((COLS, BINS), bf16),
            vm((SEQ, CH, TILE), bf16),
            vm((2, DP, SEQ, 3 * TILE), bf16),
            vm((COLS, TILE), f32),
            vm((2, DP, SEQ, 3 * TILE), bf16),
            vm((DP, COLS, TILE), f32),
            vm((3, SEQ, CH, TILE), bf16),
            vm((8, BINS), f32),
            dma((3,)),
            dma((4,)),
            dma((ZN,)),
            dma((ZN,)),
            dma((GROUP, ZN)),
            dma((GROUP, ZN)),
            dma((2, DP)),
            dma((2, DP)),
            dma((SEQ,)),
            dma((SEQ,)),
            dma((SEQ,)),
            dma((SEQ,)),
            dma((2, DP)),
            dma((2, DP)),
            dma((2, DP)),
            dma((2, DP)),
            dma((ZN,)),
            dma((ZN,)),
            dma((GROUP, ZN)),
            dma((GROUP, ZN)),
            dma((SEQ,)),
            dma((SEQ,)),
        ],
        compiler_params=pltpu.CompilerParams(
            collective_id=0, has_side_effects=True, vmem_limit_bytes=LIMIT
        ),
        name="whole",
    )(counts, w_in, b1, b2, cot, f1, f2, tables())


def body(counts, w_in, bias_one, bias_two, filter_one, filter_two, cotangent):
    out, gf1, gf2, gw, gb = whole(
        counts[0].T, w_in, bias_one, bias_two, cotangent.reshape(SEQ, CH, TILE),
        filter_one, filter_two,
    )
    return out.reshape(1, D, TILE), gw, gb[0], gb[1], gf1, gf2


def solution(mesh):
    return jax.shard_map(
        body,
        mesh=mesh,
        in_specs=(
            P("dp", "seq", None),
            P(),
            P(),
            P(),
            P("seq", "dp"),
            P("seq", "dp"),
            P("dp", None, "seq"),
        ),
        out_specs=(
            P("dp", None, "seq"),
            P(),
            P(),
            P(),
            P(("seq", "dp"), None),
            P(("seq", "dp"), None),
        ),
        check_vma=False,
    )
```

time: 800 us -> 65 us (0.08); the launches traced: 788 us -> 64.8 us
  waiting for transfers between devices: 277 us -> 0 us
  blocking collectives: 182 us -> 0 us
  other arithmetic: 116 us -> 0 us
  local copies, waits for them, and re-layouts: 92.3 us -> 6.22 us
  starting transfers between devices: 68.7 us -> 0 us
  Pallas kernels: 0 us -> 57.9 us
  matrix products: 36.2 us -> 0 us
  between operations: 15.9 us -> 0.65 us
    psum x1 -> x0, waiting for transfers between devices: 242 us -> none  [body(): lax.psum((weight_term, bias_one_term, bias_two_term), ('seq', 'dp'))]
    unnamed x9 -> x0, other arithmetic: 95.9 us -> none
    psum x1 -> x0, blocking collectives: 78.1 us -> none  [body(): lax.psum((weight_term, bias_one_term, bias_two_term), ('seq', 'dp'))]
    all_to_all x7 -> x0, starting transfers between devices: 68.6 us -> none  [the longest x3 42.1 us: to_bins(): lax.all_to_all(block.reshape(1, block.shape[0], block.shape[1]), 'seq', s...]
    pallas_call x0 -> x1, Pallas kernels: none -> 57.9 us  [whole(): pl.pallas_call(whole_kernel, out_shape=(jax.ShapeDtypeStruct((SEQ, CH, TI...]
    all_gather x2 -> x0, blocking collectives: 46.4 us -> none  [the longest x1 23.4 us: body(): lax.all_gather(filter_one, 'dp', axis=1, tiled=True)]
    unnamed x1 -> x0, blocking collectives: 40.9 us -> none
    unnamed x86 -> x10, local copies, waits for them, and re-layouts: 44.2 us -> 5.61 us
  transfers between devices with their start and end apart: 8 -> 0, of which waited for: 5 -> 0; matrix products, arithmetic and copies ran while one was open for 7% -> 0% of each run, Pallas kernels for 0% -> 0%
where the time goes in v2:
time: 65 us; the launch traced here: 64.8 us
  Pallas kernels  57.9 us (89%)
  local copies, waits for them, and re-layouts  6.22 us (10%)
  between operations  0.65 us (1%)
    pallas_call x1, Pallas kernels, whole(): pl.pallas_call(whole_kernel, out_shape=(jax.ShapeDtypeStruct((SEQ, CH, TI...  57.9 us
    unnamed x10, local copies, waits for them, and re-layouts  5.61 us

profile of v2, /device:TPU:1, one launch (start us, length us, event | category | flops | bytes accessed | tf_op | source)
XLA Modules:
  0.0 64.8 jit_solution(16199552136821905372)
XLA Ops:
  0.6 57.9 %whole.1 = (bf16[32,24,128]{2,1,0:T(8,128)(2,1)}, bf16[3,4096]{1,0:T(4,128)(2,1)}, bf16[3,4096]{1,0:T(4,128)(2,1)}, f32[64,2304]{1,0:T(8,128)}, f32[2,768]{1,0:T(2,128)}) custom-call(s32[64,128]{1,0:T(8,128)} %bitcast.7, bf16[64,2304]{1,0:T(8,128)(2,1)} %w_in.1, f32[768]{0:T(1024)} %b1_ref.1, f32[768]{0:T(1024)} %b2_ref.1, bf16[32,24,128]{2,1,0:T(8,128)(2,1)} %bitcast.5, ...), custom_call_target="tpu_custom_call" | custom-call | tf_op jit(solution)/shard_map/whole/pallas_call | solution.py:481
  58.5 0.0 copy-start.2
  58.5 0.7 %copy-done.2 = f32[2,768]{1,0:T(2,128)S(1)} copy-done((f32[2,768]{1,0:T(2,128)S(1)}, f32[2,768]{1,0:T(2,128)}, u32[]{:S(2)}) %copy-start.2) | copy-done | bytes 6168
  59.2 0.6 slice_reduce_fusion
  59.8 1.6 %copy.18 = bf16[1,768,128]{2,1,0:T(8,128)(2,1)} copy(bf16[1,768,128]{2,1,0:T(8,128)(2,1)} %bitcast.6) | data formatting | bytes 393216
  61.4 0.0 copy-start.1
  61.4 1.9 %copy.19 = f32[64,2304]{1,0:T(8,128)} copy(f32[64,2304]{1,0:T(8,128)} %get-tuple-element.25) | data formatting | bytes 1179648
  63.4 0.0 copy-done.1
  63.4 0.0 copy-start
  63.4 0.6 copy.20
  64.0 0.2 copy-done
  64.1 0.6 copy.21
Async XLA Ops:
  58.5 0.7 %copy-start.2 = (f32[2,768]{1,0:T(2,128)S(1)}, f32[2,768]{1,0:T(2,128)}, u32[]{:S(2)}) copy-start(f32[2,768]{1,0:T(2,128)} %get-tuple-element.13) | copy-start | bytes 18436
  61.4 1.9 %copy-start.1 = (bf16[3,4096]{1,0:T(4,128)(2,1)S(1)}, bf16[3,4096]{1,0:T(4,128)(2,1)}, u32[]{:S(2)}) copy-start(bf16[3,4096]{1,0:T(4,128)(2,1)} %get-tuple-element.28) | copy-start | bytes 73732
  63.4 0.8 %copy-start = (bf16[3,4096]{1,0:T(4,128)(2,1)S(1)}, bf16[3,4096]{1,0:T(4,128)(2,1)}, u32[]{:S(2)}) copy-start(bf16[3,4096]{1,0:T(4,128)(2,1)} %get-tuple-element.29) | copy-start | bytes 73732

commit v3 on v2

--- a/solution.py
+++ b/solution.py
@@ -74,10 +74,6 @@
     return s, d, s // GROUP, lax.rem(s, GROUP)
 
 
-def seq_peer(s, i):
-    return {"seq": lax.rem(s + i, SEQ)}
-
-
 def dp_peer(d, i):
     return {"dp": lax.rem(d + i, DP)}
 
@@ -97,20 +93,27 @@
     )
 
 
-def greet(s, d):
+def greet(z, q, d):
     barrier = pltpu.get_barrier_semaphore()
 
-    def hello_seq(i, _):
-        pl.semaphore_signal(barrier, inc=1, device_id=seq_peer(s, i), device_id_type=MESH)
-        return 0
-
-    def hello_dp(i, _):
-        pl.semaphore_signal(barrier, inc=1, device_id=dp_peer(d, i), device_id_type=MESH)
-        return 0
-
-    lax.fori_loop(1, SEQ, hello_seq, 0)
-    lax.fori_loop(1, DP, hello_dp, 0)
-    return lambda: pl.semaphore_wait(barrier, SEQ + DP - 2)
+    def hello(device):
+        pl.semaphore_signal(barrier, inc=1, device_id=device, device_id_type=MESH)
+
+    for i in range(1, ZN):
+        hello(z_peer(z, q, i))
+    for i in range(1, GROUP):
+        hello(q_peer(z, q, i))
+    for i in range(1, DP):
+        hello(dp_peer(d, i))
+    return lambda: pl.semaphore_wait(barrier, ZN + GROUP + DP - 3)
+
+
+def received(ref, sem, device):
+    push(ref, ref, sem, sem, device).wait_recv()
+
+
+def sent(ref, sem, device):
+    push(ref, ref, sem, sem, device).wait_send()
 
 
 def each(low, high, f):
@@ -122,23 +125,23 @@
 
 
 def whole_kernel(
-    counts_in, w_in, b1_ref, b2_ref, cot_in, f1_in, f2_in,
-    table_in,
+    counts_in, w_in, b1_in, b2_in, cot_in, f1_in, f2_in, table_in,
     outg_ref, gf1_ref, gf2_ref, gwo_ref, gb_ref,
-    counts_ref, w_ref, table, w1_ref, w2_ref, v2_ref, v1_ref, tw_ref,
-    own, wtt, wt_ref, lev_ref, cot_ref, f1_ref, f2_ref,
+    counts_ref, w_ref, table, b1_ref, b2_ref, w1_ref, w2_ref, v2_ref, v1_ref, tw_ref,
+    own, wtt, wt_ref, lev_ref, cot_mid, cot_ref, f1_ref, f2_ref,
     levs, rows, crows, val, g1, g2, hid, gm, m1, m2, gh,
-    tmp, inv, hat1, hat2, hatv, hath, hatg, gpb,
-    out_s, gf_s, gwp, gf_all, gw_in, gw_all, flat,
-    pre, loc, zs, zr, gs, gr, fs, fr, cs, cr,
-    os_, or_, hs, hr, ks, kr, azs, azr, ags, agr, vs, vr,
+    tmp, inv, hat1, hat2, hatv, hath, hatg, hat_one_grad, gpb,
+    out_s, out_mid, gf_s, gwp, gf_all, gw_in, gw_all, flat, gf_o, gw_o, gb_o,
+    pre, loc, done, zr, zs, gs, gr, fs, fr, cs, cr, os_, or_, hs, hr, ks, kr, ws, wr,
 ):
     s, d, z, q = place()
-    wait_barrier = greet(s, d)
+    wait_barrier = greet(z, q, d)
+    friend = dp_peer(d, 1)
     loads = [
         pltpu.make_async_copy(a, b, pre.at[i])
         for i, (a, b) in enumerate((
             (counts_in, counts_ref), (w_in, w_ref), (table_in, table),
+            (b1_in, b1_ref), (b2_in, b2_ref),
         ))
     ]
     for load in loads:
@@ -201,49 +204,46 @@
                 emit(2 * p + h, res[:, lanes(h)])
 
     def z_copy(i):
-        return push(own, lev_ref.at[q, z], zs.at[i], zr.at[i], z_peer(z, q, i))
+        return push(own, lev_ref.at[q, z], zs.at[0], zr.at[i], z_peer(z, q, i))
 
     def g_copy(r, i):
         slot = lev_ref.at[q, lax.rem(z - i + ZN, ZN)]
-        return push(slot, slot, gs.at[r, i], gr.at[r, i], q_peer(z, q, r))
+        return push(slot, slot, gs.at[0], gr.at[0], q_peer(z, q, r))
 
     def f_copy(i, src, dst, k):
-        return push(src, dst.at[d], fs.at[k, i], fr.at[k, i], dp_peer(d, i))
-
-    def c_copy(i):
-        return push(
-            cot_in.at[lax.rem(s + i, SEQ)], cot_ref.at[s], cs.at[i], cr.at[i], seq_peer(s, i)
-        )
-
-    def o_copy(i):
-        return push(
-            out_s.at[lax.rem(s + i, SEQ)], outg_ref.at[s], os_.at[i], or_.at[i], seq_peer(s, i)
-        )
+        return push(src, dst.at[d], fs.at[k], fr.at[k], dp_peer(d, i))
+
+    def line_copy(i, src, mid, k, send, recv):
+        to = lax.rem(z + i, ZN)
+        return push(src.at[to], mid.at[z], send.at[k], recv.at[k], z_peer(z, q, i))
+
+    def plane_copy(r, mid, dst, k, send, recv):
+        to = lax.rem(q + r, GROUP)
+        return push(mid.at[:, to], dst.at[:, q], send.at[k], recv.at[k], q_peer(z, q, r))
 
     def h_copy(which, i):
         to = lax.rem(d + i, DP)
         return push(
-            gf_s.at[which, to], gf_all.at[which, d], hs.at[which, i], hr.at[which, i],
-            dp_peer(d, i),
+            gf_s.at[which, to], gf_all.at[which, d], hs.at[which], hr.at[which], dp_peer(d, i)
         )
 
+    def part_rows(part):
+        return slice(0, CH) if part == 0 else slice(CH, COLS)
+
     def k_copy(part, i):
-        at = slice(0, CH) if part == 0 else slice(CH, COLS)
-        return push(
-            gwp.at[at], gw_in.at[d, at], ks.at[part, i], kr.at[part, i], dp_peer(d, i)
-        )
-
-    def az_copy(i):
-        slot = gw_all.at[1:3, s]
-        return push(slot, slot, azs.at[i], azr.at[i], z_peer(z, q, i))
-
-    def ag_copy(r, i):
-        slot = gw_all.at[1:3, lax.rem(z - i + ZN, ZN) * GROUP + q]
-        return push(slot, slot, ags.at[r, i], agr.at[r, i], q_peer(z, q, r))
-
-    def v_copy(i):
-        slot = gw_all.at[0, s]
-        return push(slot, slot, vs.at[i], vr.at[i], seq_peer(s, i))
+        at = part_rows(part)
+        return push(gwp.at[at], gw_in.at[d, at], ks.at[part], kr.at[part], dp_peer(d, i))
+
+    def part_blocks(part):
+        return slice(0, 1) if part == 0 else slice(1, 3)
+
+    def wz_copy(part, i):
+        slot = gw_all.at[part_blocks(part), z, q]
+        return push(slot, slot, ws.at[part], wr.at[part], z_peer(z, q, i))
+
+    def wg_copy(part, r):
+        slot = gw_all.at[part_blocks(part), :, q]
+        return push(slot, slot, ws.at[2 + part], wr.at[2 + part], q_peer(z, q, r))
 
     loads[0].wait()
     levels = jnp.log1p(counts_ref[...].astype(f32)) - 3.0
@@ -259,11 +259,10 @@
     each(1, DP, send_filters)
     for r in range(1, GROUP):
         g_copy(r, 0).start()
-    each(1, SEQ, lambda i: c_copy(i).start())
     keeps = [
         pltpu.make_async_copy(f1_in, f1_ref.at[d], loc.at[0]),
         pltpu.make_async_copy(f2_in, f2_ref.at[d], loc.at[1]),
-        pltpu.make_async_copy(cot_in.at[s], cot_ref.at[s], loc.at[2]),
+        pltpu.make_async_copy(cot_in.at[z], cot_mid.at[z], loc.at[2]),
     ]
     for keep in keeps:
         keep.start()
@@ -273,7 +272,8 @@
         at = pl.multiple_of(k * D + s * CH, 8)
         wt_ref[k * CH:(k + 1) * CH, :] = wtt[pl.ds(at, CH), :].astype(bf16)
     levs[EVENTS:, :] = jnp.zeros((TILE - EVENTS, BINS), bf16)
-    loads[2].wait()
+    for load in loads[2:]:
+        load.wait()
     for at, ref in ((0, w2_ref), (256, v2_ref)):
         hi, lo = split(table[at:at + 256, :])
         ref[0:256, :] = hi
@@ -286,12 +286,12 @@
     tw_ref[0] = table[608:640, 0:128]
     tw_ref[1] = table[608:640, 128:256]
 
-    def pass_on(i):
+    for i in (1, 7, 2, 6, 3, 5, 4):
         z_copy(i).wait_recv()
         for r in range(1, GROUP):
             g_copy(r, i).start()
-
-    each(1, ZN, pass_on)
+    for i in range(1, ZN):
+        line_copy(i, cot_in, cot_mid, 0, cs, cr).start()
 
     def load_filter(ref, dst):
         for e in range(DP):
@@ -303,19 +303,13 @@
         forward(hid, dst)
 
     keeps[0].wait()
-    each(1, DP, lambda i: f_copy(i, f1_in, f1_ref, 0).wait())
+    received(f1_ref.at[0:DP - 1], fr.at[0], friend)
     load_filter(f1_ref, hat1)
     keeps[1].wait()
-    each(1, DP, lambda i: f_copy(i, f2_in, f2_ref, 1).wait())
+    received(f2_ref.at[0:DP - 1], fr.at[1], friend)
     load_filter(f2_ref, hat2)
 
-    each(1, ZN, lambda i: z_copy(i).wait_send())
-
-    def end_group(i):
-        for r in range(1, GROUP):
-            g_copy(r, i).wait()
-
-    each(0, ZN, end_group)
+    received(lev_ref.at[0:GROUP - 1], gr.at[0], friend)
     for a in range(SEQ):
         levs[0:EVENTS, a * TILE:(a + 1) * TILE] = lev_ref[a % GROUP, a // GROUP]
     for p in range(SEQ // 2):
@@ -327,6 +321,12 @@
         val[:, lanes(c)] = rows[pl.ds(c, SEQ, stride=COLS), :].astype(bf16)
         g1[:, lanes(c)] = rows[pl.ds(CH + c, SEQ, stride=COLS), :].astype(bf16)
         g2[:, lanes(c)] = rows[pl.ds(2 * CH + c, SEQ, stride=COLS), :].astype(bf16)
+    keeps[2].wait()
+    received(cot_mid.at[0:ZN - 1], cr.at[0], friend)
+    for r in range(1, GROUP):
+        plane_copy(r, cot_mid, cot_ref, 1, cs, cr).start()
+    keep_cot = pltpu.make_async_copy(cot_mid.at[:, q], cot_ref.at[:, q], loc.at[3])
+    keep_cot.start()
     forward(val, hatv)
 
     def emit_one(c, conv):
@@ -337,10 +337,10 @@
     inverse(hat1, hatv, False, emit_one)
     forward(hid, hath)
 
-    keeps[2].wait()
-    each(1, SEQ, lambda i: c_copy(i).wait())
+    keep_cot.wait()
+    received(cot_ref.at[:, 0:GROUP - 1], cr.at[1], friend)
     for a in range(SEQ):
-        crows[a * CH:(a + 1) * CH, :] = cot_ref[a].astype(f32)
+        crows[a * CH:(a + 1) * CH, :] = cot_ref[a // GROUP, a % GROUP].astype(f32)
 
     def emit_two(c, conv):
         mixed = rnd(conv) + b2_ref[base + c] * hid[:, lanes(c)].astype(f32)
@@ -354,9 +354,10 @@
     for c in range(CH):
         crows[pl.ds(c, SEQ, stride=CH), :] = m2[:, lanes(c)]
     for a in range(SEQ):
-        out_s[a] = crows[a * CH:(a + 1) * CH, :].astype(bf16)
-    each(1, SEQ, lambda i: o_copy(i).start())
-    keep_out = pltpu.make_async_copy(out_s.at[s], outg_ref.at[s], loc.at[3])
+        out_s[a // GROUP, a % GROUP] = crows[a * CH:(a + 1) * CH, :].astype(bf16)
+    for i in range(1, ZN):
+        line_copy(i, out_s, out_mid, 0, os_, or_).start()
+    keep_out = pltpu.make_async_copy(out_s.at[z], out_mid.at[z], loc.at[4])
     keep_out.start()
 
     def bias_sums(x_ref, y_ref):
@@ -383,22 +384,30 @@
         for k in range(1, DP):
             total = total + gw_in[k, low:high, :]
         for k in range(low // CH, high // CH):
-            gw_all[k, s] = total[k * CH - low:(k + 1) * CH - low].astype(bf16)
+            gw_all[k, z, q] = total[k * CH - low:(k + 1) * CH - low].astype(bf16)
 
     def emit_gf(which):
         def emit(c, conv):
             gf_s[which, c // 3, :, (c % 3) * TILE:(c % 3 + 1) * TILE] = conv.astype(bf16)
         return emit
 
+    gives = []
+
+    def give(src, dst, k):
+        copy = pltpu.make_async_copy(src, dst, done.at[k])
+        copy.start()
+        gives.append(copy)
+
     def finish_filter(which, dst):
-        each(1, DP, lambda i: h_copy(which, i).wait())
+        received(gf_all.at[which, 0:DP - 1], hr.at[which], friend)
         total = gf_all[which, 0].astype(f32)
         for k in range(1, DP):
             total = total + gf_all[which, k].astype(f32)
         for c in range(3):
             for a in range(SEQ):
                 flat[c:c + 1, a * TILE:(a + 1) * TILE] = total[a:a + 1, lanes(c)]
-        dst[...] = flat[0:3, :].astype(bf16)
+        gf_o[which] = flat[0:3, :].astype(bf16)
+        give(gf_o.at[which], dst, which)
 
     forward(gm, hatg)
     sum_two = bias_sums(gm, hid)
@@ -410,13 +419,10 @@
 
     inverse(hat2, hatg, True, emit_carried_two)
     weight_rows(CH, COLS, jnp.concatenate([sum_two, jnp.zeros((CH, 1), f32)], axis=0))
-    each(1, DP, lambda i: k_copy(1, i).start())
-
-    inverse(hath, hatg, True, emit_gf(1))
-    gf_all[1, d] = gf_s[1, d]
-    each(1, DP, lambda i: h_copy(1, i).start())
-
-    forward(gh, hatg)
+    for i in range(1, DP):
+        k_copy(1, i).start()
+
+    forward(gh, hat_one_grad)
     sum_one = bias_sums(gh, val)
 
     def emit_carried_one(c, conv):
@@ -424,54 +430,80 @@
             b1_ref[base + c] * gh[:, lanes(c)].astype(f32) + rnd(conv)
         )
 
-    inverse(hat1, hatg, True, emit_carried_one)
+    inverse(hat1, hat_one_grad, True, emit_carried_one)
     weight_rows(0, CH, sum_one)
-    each(1, DP, lambda i: k_copy(0, i).start())
-
-    each(1, DP, lambda i: k_copy(1, i).wait())
+    for i in range(1, DP):
+        k_copy(0, i).start()
+
+    inverse(hath, hatg, True, emit_gf(1))
+    gf_all[1, d] = gf_s[1, d]
+    for i in range(1, DP):
+        h_copy(1, i).start()
+
+    received(gw_in.at[0:DP - 1, part_rows(1)], kr.at[1], friend)
     total_rows(CH, COLS)
-    each(1, ZN, lambda i: az_copy(i).start())
+    for i in range(1, ZN):
+        wz_copy(1, i).start()
+    keep_out.wait()
+    received(out_mid.at[0:ZN - 1], or_.at[0], friend)
     for r in range(1, GROUP):
-        ag_copy(r, 0).start()
-
-    inverse(hatv, hatg, True, emit_gf(0))
+        plane_copy(r, out_mid, outg_ref, 1, os_, or_).start()
+    keep_plane = pltpu.make_async_copy(out_mid.at[:, q], outg_ref.at[:, q], loc.at[5])
+    keep_plane.start()
+
+    inverse(hatv, hat_one_grad, True, emit_gf(0))
     gf_all[0, d] = gf_s[0, d]
-    each(1, DP, lambda i: h_copy(0, i).start())
-
-    each(1, DP, lambda i: k_copy(0, i).wait())
+    for i in range(1, DP):
+        h_copy(0, i).start()
+
+    received(gw_in.at[0:DP - 1, part_rows(0)], kr.at[0], friend)
     total_rows(0, CH)
-    each(1, SEQ, lambda i: v_copy(i).start())
-
-    def pass_on_weights(i):
-        az_copy(i).wait_recv()
-        for r in range(1, GROUP):
-            ag_copy(r, i).start()
-
-    each(1, ZN, pass_on_weights)
-    finish_filter(1, gf2_ref)
-    finish_filter(0, gf1_ref)
-    each(1, ZN, lambda i: az_copy(i).wait_send())
-
-    def end_weights(i):
-        for r in range(1, GROUP):
-            ag_copy(r, i).wait()
+    for i in range(1, ZN):
+        wz_copy(0, i).start()
 
     def turn(k):
         block = gw_all[k].astype(f32).reshape(D, TILE)
         for p in range(D // TILE):
             turned = block[p * TILE:(p + 1) * TILE, :].T
             at = k * D + p * TILE
-            gwo_ref[:, at:at + TILE] = turned[0:EVENTS, :]
+            gw_o[:, at:at + TILE] = turned[0:EVENTS, :]
             if k < 2:
-                gb_ref[k:k + 1, p * TILE:(p + 1) * TILE] = turned[EVENTS:EVENTS + 1, :]
-
-    each(0, ZN, end_weights)
+                gb_o[k:k + 1, p * TILE:(p + 1) * TILE] = turned[EVENTS:EVENTS + 1, :]
+        at = slice(k * D, (k + 1) * D)
+        give(gw_o.at[:, at], gwo_ref.at[:, at], 2 + k)
+
+    def pass_weights(part):
+        received(gw_all.at[part_blocks(part), 0:ZN - 1, 0], wr.at[part], friend)
+        for r in range(1, GROUP):
+            wg_copy(part, r).start()
+
+    pass_weights(1)
+    finish_filter(1, gf2_ref)
+    pass_weights(0)
+    finish_filter(0, gf1_ref)
+    received(gw_all.at[part_blocks(1), :, 0:GROUP - 1], wr.at[3], friend)
     turn(1)
     turn(2)
-    each(1, SEQ, lambda i: v_copy(i).wait())
+    received(gw_all.at[part_blocks(0), :, 0:GROUP - 1], wr.at[2], friend)
     turn(0)
-    keep_out.wait()
-    each(1, SEQ, lambda i: o_copy(i).wait())
+    give(gb_o, gb_ref, 5)
+    keep_plane.wait()
+    received(outg_ref.at[:, 0:GROUP - 1], or_.at[1], friend)
+    sent(lev_ref.at[0, 0:ZN - 1], zs.at[0], friend)
+    sent(lev_ref.at[0:GROUP - 1], gs.at[0], friend)
+    sent(f1_ref.at[0:DP - 1], fs.at[0], friend)
+    sent(f2_ref.at[0:DP - 1], fs.at[1], friend)
+    sent(cot_mid.at[0:ZN - 1], cs.at[0], friend)
+    sent(cot_ref.at[:, 0:GROUP - 1], cs.at[1], friend)
+    sent(out_mid.at[0:ZN - 1], os_.at[0], friend)
+    sent(outg_ref.at[:, 0:GROUP - 1], os_.at[1], friend)
+    for part in range(2):
+        sent(gf_all.at[part, 0:DP - 1], hs.at[part], friend)
+        sent(gw_in.at[0:DP - 1, part_rows(part)], ks.at[part], friend)
+        sent(gw_all.at[part_blocks(part), 0:ZN - 1, 0], ws.at[part], friend)
+        sent(gw_all.at[part_blocks(part), :, 0:GROUP - 1], ws.at[2 + part], friend)
+    for copy in gives:
+        copy.wait()
 
 
 def whole(counts, w_in, b1, b2, cot, f1, f2):
@@ -481,18 +513,20 @@
     return pl.pallas_call(
         whole_kernel,
         out_shape=(
-            jax.ShapeDtypeStruct((SEQ, CH, TILE), bf16),
+            jax.ShapeDtypeStruct((ZN, GROUP, CH, TILE), bf16),
             jax.ShapeDtypeStruct((3, BINS), bf16),
             jax.ShapeDtypeStruct((3, BINS), bf16),
             jax.ShapeDtypeStruct((EVENTS, 3 * D), f32),
             jax.ShapeDtypeStruct((2, D), f32),
         ),
-        in_specs=[ANY, ANY, SMEM, SMEM] + [ANY] * 4,
-        out_specs=(ANY, VMEM, VMEM, VMEM, VMEM),
+        in_specs=[ANY] * 8,
+        out_specs=(ANY,) * 5,
         scratch_shapes=[
             vm((EVENTS, TILE), jnp.int32),
             vm((EVENTS, 3 * D), bf16),
             vm((640, 2 * TILE), f32),
+            pltpu.SMEM((D,), f32),
+            pltpu.SMEM((D,), f32),
             vm((2 * SEQ, 2 * SEQ), bf16),
             vm((6 * TILE, 2 * TILE), bf16),
             vm((6 * TILE, 2 * TILE), bf16),
@@ -502,7 +536,8 @@
             vm((3 * D, EVENTS), f32),
             vm((COLS, EVENTS), bf16),
             vm((GROUP, ZN, EVENTS, TILE), bf16),
-            vm((SEQ, CH, TILE), bf16),
+            vm((ZN, GROUP, CH, TILE), bf16),
+            vm((ZN, GROUP, CH, TILE), bf16),
             vm((DP, CH, BINS // DP), bf16),
             vm((DP, CH, BINS // DP), bf16),
             vm((TILE, BINS), bf16),
@@ -523,36 +558,38 @@
             vm(spec, f32),
             vm(spec, f32),
             vm(spec, f32),
+            vm(spec, f32),
             vm((COLS, BINS), bf16),
-            vm((SEQ, CH, TILE), bf16),
+            vm((ZN, GROUP, CH, TILE), bf16),
+            vm((ZN, GROUP, CH, TILE), bf16),
             vm((2, DP, SEQ, 3 * TILE), bf16),
             vm((COLS, TILE), f32),
             vm((2, DP, SEQ, 3 * TILE), bf16),
             vm((DP, COLS, TILE), f32),
-            vm((3, SEQ, CH, TILE), bf16),
+            vm((3, ZN, GROUP, CH, TILE), bf16),
             vm((8, BINS), f32),
-            dma((3,)),
+            vm((2, 3, BINS), bf16),
+            vm((EVENTS, 3 * D), f32),
+            vm((2, D), f32),
+            dma((5,)),
+            dma((6,)),
+            dma((6,)),
+            dma((8,)),
+            dma((1,)),
+            dma((1,)),
+            dma((1,)),
+            dma((2,)),
+            dma((2,)),
+            dma((2,)),
+            dma((2,)),
+            dma((2,)),
+            dma((2,)),
+            dma((2,)),
+            dma((2,)),
+            dma((2,)),
+            dma((2,)),
             dma((4,)),
-            dma((ZN,)),
-            dma((ZN,)),
-            dma((GROUP, ZN)),
-            dma((GROUP, ZN)),
-            dma((2, DP)),
-            dma((2, DP)),
-            dma((SEQ,)),
-            dma((SEQ,)),
-            dma((SEQ,)),
-            dma((SEQ,)),
-            dma((2, DP)),
-            dma((2, DP)),
-            dma((2, DP)),
-            dma((2, DP)),
-            dma((ZN,)),
-            dma((ZN,)),
-            dma((GROUP, ZN)),
-            dma((GROUP, ZN)),
-            dma((SEQ,)),
-            dma((SEQ,)),
+            dma((4,)),
         ],
         compiler_params=pltpu.CompilerParams(
             collective_id=0, has_side_effects=True, vmem_limit_bytes=LIMIT
@@ -561,12 +598,37 @@
     )(counts, w_in, b1, b2, cot, f1, f2, tables())
 
 
+def finish_kernel(
+    out_in, gf1_in, gf2_in, gw_in, gb_in, out_ref, gf1_ref, gf2_ref, gw_ref, gb1_ref, gb2_ref
+):
+    out_ref[...] = out_in[...]
+    gf1_ref[...] = gf1_in[...]
+    gf2_ref[...] = gf2_in[...]
+    gw_ref[...] = gw_in[...]
+    gb1_ref[...] = gb_in[0]
+    gb2_ref[...] = gb_in[1]
+
+
+def finish(out, gf1, gf2, gw, gb):
+    like = [jax.ShapeDtypeStruct(x.shape, x.dtype) for x in (out, gf1, gf2, gw)]
+    flat = jax.ShapeDtypeStruct((D,), f32)
+    return pl.pallas_call(
+        finish_kernel,
+        out_shape=(*like, flat, flat),
+        in_specs=[VMEM] * 5,
+        out_specs=(VMEM,) * 6,
+        compiler_params=pltpu.CompilerParams(vmem_limit_bytes=LIMIT),
+        name="finish",
+    )(out, gf1, gf2, gw, gb)
+
+
 def body(counts, w_in, bias_one, bias_two, filter_one, filter_two, cotangent):
     out, gf1, gf2, gw, gb = whole(
-        counts[0].T, w_in, bias_one, bias_two, cotangent.reshape(SEQ, CH, TILE),
+        counts[0].T, w_in, bias_one, bias_two, cotangent.reshape(ZN, GROUP, CH, TILE),
         filter_one, filter_two,
     )
-    return out.reshape(1, D, TILE), gw, gb[0], gb[1], gf1, gf2
+    out, gf1, gf2, gw, gb1, gb2 = finish(out.reshape(1, D, TILE), gf1, gf2, gw, gb)
+    return out, gw, gb1, gb2, gf1, gf2
 
 
 def solution(mesh):

time: 65 us -> 53.5 us (0.82)
  local copies, waits for them, and re-layouts: 6.22 us -> 0 us
  Pallas kernels: 57.9 us -> 52.7 us
    unnamed x10 -> x0, local copies, waits for them, and re-layouts: 5.61 us -> none
    pallas_call x1 -> x2, Pallas kernels: 57.9 us -> 52.7 us  [the longest x1 50.7 us: whole(): pl.pallas_call(whole_kernel, out_shape=(jax.ShapeDtypeStruct((ZN, GROUP,...]
where the time goes in v3:
time: 53.5 us; the launch traced here: 53.4 us
  Pallas kernels  52.7 us (99%)
  between operations  0.64 us (1%)
    pallas_call x1, Pallas kernels, whole(): pl.pallas_call(whole_kernel, out_shape=(jax.ShapeDtypeStruct((ZN, GROUP,...  50.7 us
    pallas_call x1, Pallas kernels, finish(): pl.pallas_call(finish_kernel, out_shape=(*like, flat, flat), in_specs=[VM...  2.05 us

profile of v3, /device:TPU:1, one launch (start us, length us, event | category | flops | bytes accessed | tf_op | source)
XLA Modules:
  0.0 53.4 jit_solution(13939881863896662048)
XLA Ops:
  0.6 50.7 %whole.1 = (bf16[8,4,24,128]{3,2,1,0:T(8,128)(2,1)}, bf16[3,4096]{1,0:T(4,128)(2,1)}, bf16[3,4096]{1,0:T(4,128)(2,1)}, f32[64,2304]{1,0:T(8,128)}, f32[2,768]{1,0:T(2,128)}) custom-call(s32[64,128]{1,0:T(8,128)} %bitcast.7, bf16[64,2304]{1,0:T(8,128)(2,1)} %w_in.1, f32[768]{0:T(1024)} %b1_in.1, f32[768]{0:T(1024)} %b2_in.1, bf16[8,4,24,128]{3,2,1,0:T(8,128)(2,1)} %bitcast.5, ...), custom_call_target="tpu_custom_call" | custom-call | tf_op jit(solution)/shard_map/whole/pallas_call | solution.py:513
  51.3 2.1 %finish.1 = (bf16[1,768,128]{2,1,0:T(8,128)(2,1)}, bf16[3,4096]{1,0:T(4,128)(2,1)}, bf16[3,4096]{1,0:T(4,128)(2,1)}, f32[64,2304]{1,0:T(8,128)}, f32[768]{0:T(1024)}, /*index=5*/f32[768]{0:T(1024)}) custom-call(bf16[1,768,128]{2,1,0:T(8,128)(2,1)} %bitcast.6, bf16[3,4096]{1,0:T(4,128)(2,1)} %get-tuple-element.18.gf1_in, ...), custom_call_target="tpu_custom_call" | custom-call | tf_op jit(solution)/shard_map/finish/pallas_call | solution.py:615

commit v4 on v3

--- a/solution.py
+++ b/solution.py
@@ -27,6 +27,8 @@
 SMEM = pl.BlockSpec(memory_space=pltpu.SMEM)
 ANY = pl.BlockSpec(memory_space=pl.ANY)
 LIMIT = 56 * 1024 * 1024
+LINE = (4, 3, 5, 2, 6, 1, 7)
+FAR = (8, 7, 9, 6, 10, 5, 11, 4, 12, 3, 13, 2, 14, 1, 15)
 
 
 def tables():
@@ -93,19 +95,30 @@
     )
 
 
-def greet(z, q, d):
+def same_core(s, i):
+    return {"seq": lax.rem(s + 2 * i, SEQ)}
+
+
+def core_peer(s):
+    return {"seq": s + 1 - 2 * lax.rem(s, 2)}
+
+
+def pair(d):
+    return d + 1 - 2 * lax.rem(d, 2)
+
+
+def greet(s, z, q, d):
     barrier = pltpu.get_barrier_semaphore()
 
     def hello(device):
         pl.semaphore_signal(barrier, inc=1, device_id=device, device_id_type=MESH)
 
-    for i in range(1, ZN):
-        hello(z_peer(z, q, i))
-    for i in range(1, GROUP):
-        hello(q_peer(z, q, i))
+    for i in range(1, SEQ // 2):
+        hello(same_core(s, i))
+    hello(core_peer(s))
     for i in range(1, DP):
         hello(dp_peer(d, i))
-    return lambda: pl.semaphore_wait(barrier, ZN + GROUP + DP - 3)
+    return lambda: pl.semaphore_wait(barrier, SEQ // 2 + DP - 1)
 
 
 def received(ref, sem, device):
@@ -131,12 +144,15 @@
     own, wtt, wt_ref, lev_ref, cot_mid, cot_ref, f1_ref, f2_ref,
     levs, rows, crows, val, g1, g2, hid, gm, m1, m2, gh,
     tmp, inv, hat1, hat2, hatv, hath, hatg, hat_one_grad, gpb,
-    out_s, out_mid, gf_s, gwp, gf_all, gw_in, gw_all, flat, gf_o, gw_o, gb_o,
-    pre, loc, done, zr, zs, gs, gr, fs, fr, cs, cr, os_, or_, hs, hr, ks, kr, ws, wr,
+    out_s, out_mid, gf_s, gwp, gf_all, gw_in, gw_v, gw_g, flat, gf_o, gw_o, gb_o,
+    pre, loc, done, zr, xr, zs, gs, gr, fs, fr, cs, cr, os_, or_, hs, hr, ks, kr, ws, wr,
 ):
     s, d, z, q = place()
-    wait_barrier = greet(z, q, d)
+    m = s // 2
+    core = lax.rem(s, 2)
+    wait_barrier = greet(s, z, q, d)
     friend = dp_peer(d, 1)
+    gw_all = (gw_v, gw_g)
     loads = [
         pltpu.make_async_copy(a, b, pre.at[i])
         for i, (a, b) in enumerate((
@@ -206,20 +222,32 @@
     def z_copy(i):
         return push(own, lev_ref.at[q, z], zs.at[0], zr.at[i], z_peer(z, q, i))
 
-    def g_copy(r, i):
+    def x_copy(i):
         slot = lev_ref.at[q, lax.rem(z - i + ZN, ZN)]
-        return push(slot, slot, gs.at[0], gr.at[0], q_peer(z, q, r))
+        return push(slot, slot, gs.at[0], xr.at[i], q_peer(z, q, 2))
+
+    def g_copy(k, i):
+        slot = lev_ref.at[lax.rem(q + k, GROUP), lax.rem(z - i + ZN, ZN)]
+        return push(slot, slot, gs.at[0], gr.at[0], core_peer(s))
 
     def f_copy(i, src, dst, k):
-        return push(src, dst.at[d], fs.at[k], fr.at[k], dp_peer(d, i))
-
-    def line_copy(i, src, mid, k, send, recv):
-        to = lax.rem(z + i, ZN)
-        return push(src.at[to], mid.at[z], send.at[k], recv.at[k], z_peer(z, q, i))
-
-    def plane_copy(r, mid, dst, k, send, recv):
-        to = lax.rem(q + r, GROUP)
-        return push(mid.at[:, to], dst.at[:, q], send.at[k], recv.at[k], q_peer(z, q, r))
+        return push(src, dst.at[d], fs.at[k], fr.at[k], dp_peer(d, 2 * i))
+
+    def fx_copy(src, dst, k):
+        return push(src, dst.at[d], fs.at[k], fr.at[2 + k], {"dp": pair(d)})
+
+    def fy_copy(i, dst, k):
+        slot = dst.at[pair(d)]
+        return push(slot, slot, fs.at[k], fr.at[k], dp_peer(d, 2 * i))
+
+    def far_copy(i, src, mid, k, send, recv):
+        to = lax.rem(m + i, SEQ // 2)
+        return push(src.at[to], mid.at[m], send.at[k], recv.at[k], same_core(s, i))
+
+    def near_copy(mid, dst, k, send, recv):
+        return push(
+            mid.at[:, 1 - core], dst.at[:, core], send.at[k], recv.at[k], core_peer(s)
+        )
 
     def h_copy(which, i):
         to = lax.rem(d + i, DP)
@@ -228,41 +256,41 @@
         )
 
     def part_rows(part):
-        return slice(0, CH) if part == 0 else slice(CH, COLS)
+        return slice(0, 16) if part == 0 else slice(16, 40)
 
     def k_copy(part, i):
         at = part_rows(part)
         return push(gwp.at[at], gw_in.at[d, at], ks.at[part], kr.at[part], dp_peer(d, i))
 
-    def part_blocks(part):
-        return slice(0, 1) if part == 0 else slice(1, 3)
-
     def wz_copy(part, i):
-        slot = gw_all.at[part_blocks(part), z, q]
-        return push(slot, slot, ws.at[part], wr.at[part], z_peer(z, q, i))
-
-    def wg_copy(part, r):
-        slot = gw_all.at[part_blocks(part), :, q]
-        return push(slot, slot, ws.at[2 + part], wr.at[2 + part], q_peer(z, q, r))
+        slot = gw_all[part].at[m, core]
+        return push(slot, slot, ws.at[part], wr.at[part], same_core(s, i))
+
+    def wg_copy(part):
+        slot = gw_all[part].at[:, core]
+        return push(slot, slot, ws.at[2 + part], wr.at[2 + part], core_peer(s))
 
     loads[0].wait()
     levels = jnp.log1p(counts_ref[...].astype(f32)) - 3.0
     own[...] = levels.astype(bf16)
     lev_ref[q, z] = own[...]
     wait_barrier()
-    each(1, ZN, lambda i: z_copy(i).start())
-
-    def send_filters(i):
+    for i in LINE:
+        z_copy(i).start()
+
+    for i in FAR:
+        far_copy(i, cot_in, cot_mid, 0, cs, cr).start()
+    fx_copy(f1_in, f1_ref, 0).start()
+    fx_copy(f2_in, f2_ref, 1).start()
+    x_copy(0).start()
+    g_copy(0, 0).start()
+    for i in range(1, DP // 2):
         f_copy(i, f1_in, f1_ref, 0).start()
         f_copy(i, f2_in, f2_ref, 1).start()
-
-    each(1, DP, send_filters)
-    for r in range(1, GROUP):
-        g_copy(r, 0).start()
     keeps = [
         pltpu.make_async_copy(f1_in, f1_ref.at[d], loc.at[0]),
         pltpu.make_async_copy(f2_in, f2_ref.at[d], loc.at[1]),
-        pltpu.make_async_copy(cot_in.at[z], cot_mid.at[z], loc.at[2]),
+        pltpu.make_async_copy(cot_in.at[m], cot_mid.at[m], loc.at[2]),
     ]
     for keep in keeps:
         keep.start()
@@ -286,12 +314,17 @@
     tw_ref[0] = table[608:640, 0:128]
     tw_ref[1] = table[608:640, 128:256]
 
-    for i in (1, 7, 2, 6, 3, 5, 4):
+    for i in LINE:
         z_copy(i).wait_recv()
-        for r in range(1, GROUP):
-            g_copy(r, i).start()
-    for i in range(1, ZN):
-        line_copy(i, cot_in, cot_mid, 0, cs, cr).start()
+        x_copy(i).start()
+        g_copy(0, i).start()
+    for ref, k in ((f1_ref, 0), (f2_ref, 1)):
+        received(ref.at[0], fr.at[2 + k], friend)
+        for j in range(1, DP // 2):
+            fy_copy(j, ref, k).start()
+    for i in (0, *LINE):
+        x_copy(i).wait_recv()
+        g_copy(2, i).start()
 
     def load_filter(ref, dst):
         for e in range(DP):
@@ -303,13 +336,13 @@
         forward(hid, dst)
 
     keeps[0].wait()
-    received(f1_ref.at[0:DP - 1], fr.at[0], friend)
+    received(f1_ref.at[0:DP - 2], fr.at[0], friend)
     load_filter(f1_ref, hat1)
     keeps[1].wait()
-    received(f2_ref.at[0:DP - 1], fr.at[1], friend)
+    received(f2_ref.at[0:DP - 2], fr.at[1], friend)
     load_filter(f2_ref, hat2)
 
-    received(lev_ref.at[0:GROUP - 1], gr.at[0], friend)
+    received(lev_ref.at[0:2], gr.at[0], friend)
     for a in range(SEQ):
         levs[0:EVENTS, a * TILE:(a + 1) * TILE] = lev_ref[a % GROUP, a // GROUP]
     for p in range(SEQ // 2):
@@ -322,10 +355,9 @@
         g1[:, lanes(c)] = rows[pl.ds(CH + c, SEQ, stride=COLS), :].astype(bf16)
         g2[:, lanes(c)] = rows[pl.ds(2 * CH + c, SEQ, stride=COLS), :].astype(bf16)
     keeps[2].wait()
-    received(cot_mid.at[0:ZN - 1], cr.at[0], friend)
-    for r in range(1, GROUP):
-        plane_copy(r, cot_mid, cot_ref, 1, cs, cr).start()
-    keep_cot = pltpu.make_async_copy(cot_mid.at[:, q], cot_ref.at[:, q], loc.at[3])
+    received(cot_mid.at[0:SEQ // 2 - 1], cr.at[0], friend)
+    near_copy(cot_mid, cot_ref, 1, cs, cr).start()
+    keep_cot = pltpu.make_async_copy(cot_mid.at[:, core], cot_ref.at[:, core], loc.at[3])
     keep_cot.start()
     forward(val, hatv)
 
@@ -338,9 +370,9 @@
     forward(hid, hath)
 
     keep_cot.wait()
-    received(cot_ref.at[:, 0:GROUP - 1], cr.at[1], friend)
+    received(cot_ref.at[:, 0], cr.at[1], friend)
     for a in range(SEQ):
-        crows[a * CH:(a + 1) * CH, :] = cot_ref[a // GROUP, a % GROUP].astype(f32)
+        crows[a * CH:(a + 1) * CH, :] = cot_ref[a // 2, a % 2].astype(f32)
 
     def emit_two(c, conv):
         mixed = rnd(conv) + b2_ref[base + c] * hid[:, lanes(c)].astype(f32)
@@ -354,10 +386,10 @@
     for c in range(CH):
         crows[pl.ds(c, SEQ, stride=CH), :] = m2[:, lanes(c)]
     for a in range(SEQ):
-        out_s[a // GROUP, a % GROUP] = crows[a * CH:(a + 1) * CH, :].astype(bf16)
-    for i in range(1, ZN):
-        line_copy(i, out_s, out_mid, 0, os_, or_).start()
-    keep_out = pltpu.make_async_copy(out_s.at[z], out_mid.at[z], loc.at[4])
+        out_s[a // 2, a % 2] = crows[a * CH:(a + 1) * CH, :].astype(bf16)
+    for i in FAR:
+        far_copy(i, out_s, out_mid, 0, os_, or_).start()
+    keep_out = pltpu.make_async_copy(out_s.at[m], out_mid.at[m], loc.at[4])
     keep_out.start()
 
     def bias_sums(x_ref, y_ref):
@@ -367,7 +399,8 @@
             parts.append(jnp.sum(t, axis=0, keepdims=True))
         return jnp.sum(jnp.concatenate(parts, axis=0), axis=1, keepdims=True)
 
-    def weight_rows(low, high, sums):
+    def weight_rows(part, sums):
+        low, high = ((0, CH), (CH, COLS))[part]
         for a in range(SEQ):
             gpb[low:high, a * TILE:(a + 1) * TILE] = rows[
                 a * COLS + low:a * COLS + high, :
@@ -375,16 +408,26 @@
         weight = lax.dot_general(
             gpb[low:high, :], levs[...], (((1,), (1,)), ((), ())), preferred_element_type=f32
         )
-        lane = lax.broadcasted_iota(jnp.int32, (high - low, TILE), 1)
-        gwp[low:high, :] = weight + jnp.where(lane == EVENTS, sums, 0.0)
-        gw_in[d, low:high, :] = gwp[low:high, :]
-
-    def total_rows(low, high):
-        total = gw_in[0, low:high, :]
+        packed = [
+            weight[r:r + 8] + pltpu.roll(weight[r + 8:r + 16], EVENTS, 1)
+            for r in range(0, high - low - 8, 16)
+        ]
+        if part == 0:
+            lane = lax.broadcasted_iota(jnp.int32, (8, TILE), 1)
+            last = weight[16:24]
+            for k, total in enumerate(sums):
+                for r in range(3):
+                    last = jnp.where(lane == EVENTS + 3 * k + r, total[8 * r:8 * r + 8], last)
+            packed.append(last)
+        packed = jnp.concatenate(packed, axis=0)
+        gwp[part_rows(part), :] = packed
+        gw_in[d, part_rows(part), :] = packed
+
+    def total_rows(part):
+        total = gw_in[0, part_rows(part), :]
         for k in range(1, DP):
-            total = total + gw_in[k, low:high, :]
-        for k in range(low // CH, high // CH):
-            gw_all[k, z, q] = total[k * CH - low:(k + 1) * CH - low].astype(bf16)
+            total = total + gw_in[k, part_rows(part), :]
+        gw_all[part][m, core] = total.astype(bf16)
 
     def emit_gf(which):
         def emit(c, conv):
@@ -418,7 +461,7 @@
         rows[pl.ds(CH + c, SEQ, stride=COLS), :] = ghid * m1[:, lanes(c)]
 
     inverse(hat2, hatg, True, emit_carried_two)
-    weight_rows(CH, COLS, jnp.concatenate([sum_two, jnp.zeros((CH, 1), f32)], axis=0))
+    weight_rows(1, ())
     for i in range(1, DP):
         k_copy(1, i).start()
 
@@ -431,7 +474,7 @@
         )
 
     inverse(hat1, hat_one_grad, True, emit_carried_one)
-    weight_rows(0, CH, sum_one)
+    weight_rows(0, (sum_one, sum_two))
     for i in range(1, DP):
         k_copy(0, i).start()
 
@@ -441,67 +484,82 @@
         h_copy(1, i).start()
 
     received(gw_in.at[0:DP - 1, part_rows(1)], kr.at[1], friend)
-    total_rows(CH, COLS)
-    for i in range(1, ZN):
+    total_rows(1)
+    for i in FAR:
         wz_copy(1, i).start()
-    keep_out.wait()
-    received(out_mid.at[0:ZN - 1], or_.at[0], friend)
-    for r in range(1, GROUP):
-        plane_copy(r, out_mid, outg_ref, 1, os_, or_).start()
-    keep_plane = pltpu.make_async_copy(out_mid.at[:, q], outg_ref.at[:, q], loc.at[5])
-    keep_plane.start()
-
     inverse(hatv, hat_one_grad, True, emit_gf(0))
     gf_all[0, d] = gf_s[0, d]
     for i in range(1, DP):
         h_copy(0, i).start()
 
+    keep_out.wait()
+    received(out_mid.at[0:SEQ // 2 - 1], or_.at[0], friend)
+    near_copy(out_mid, outg_ref, 1, os_, or_).start()
+    keep_plane = pltpu.make_async_copy(out_mid.at[:, core], outg_ref.at[:, core], loc.at[5])
+    keep_plane.start()
     received(gw_in.at[0:DP - 1, part_rows(0)], kr.at[0], friend)
-    total_rows(0, CH)
-    for i in range(1, ZN):
+    total_rows(0)
+    for i in FAR:
         wz_copy(0, i).start()
 
     def turn(k):
-        block = gw_all[k].astype(f32).reshape(D, TILE)
+        low = lax.broadcasted_iota(jnp.int32, (8, TILE), 1) < EVENTS
+        block = []
+        for n in range(SEQ):
+            b = gw_all[min(k, 1)][n // 2, n % 2].astype(f32)
+            tiles = [b[r:r + 8] for r in range(0, b.shape[0], 8)]
+            if k == 0:
+                first, last = tiles
+                block.append(jnp.where(low, first, last))
+                block.append(
+                    jnp.where(low, pltpu.roll(first, EVENTS, 1), pltpu.roll(last, TILE - 1, 1))
+                )
+                block.append(jnp.where(low, last, pltpu.roll(last, TILE - 2, 1)))
+            elif k == 1:
+                block += [tiles[0], pltpu.roll(tiles[0], EVENTS, 1), tiles[1]]
+            else:
+                block += [
+                    pltpu.roll(tiles[1], EVENTS, 1), tiles[2], pltpu.roll(tiles[2], EVENTS, 1)
+                ]
         for p in range(D // TILE):
-            turned = block[p * TILE:(p + 1) * TILE, :].T
+            turned = jnp.concatenate(block[16 * p:16 * p + 16], axis=0).T
             at = k * D + p * TILE
             gw_o[:, at:at + TILE] = turned[0:EVENTS, :]
-            if k < 2:
-                gb_o[k:k + 1, p * TILE:(p + 1) * TILE] = turned[EVENTS:EVENTS + 1, :]
+            if k == 0:
+                gb_o[0:1, p * TILE:(p + 1) * TILE] = turned[EVENTS:EVENTS + 1, :]
+                gb_o[1:2, p * TILE:(p + 1) * TILE] = turned[EVENTS + 3:EVENTS + 4, :]
         at = slice(k * D, (k + 1) * D)
         give(gw_o.at[:, at], gwo_ref.at[:, at], 2 + k)
 
     def pass_weights(part):
-        received(gw_all.at[part_blocks(part), 0:ZN - 1, 0], wr.at[part], friend)
-        for r in range(1, GROUP):
-            wg_copy(part, r).start()
+        received(gw_all[part].at[0:SEQ // 2 - 1, 0], wr.at[part], friend)
+        wg_copy(part).start()
 
     pass_weights(1)
     finish_filter(1, gf2_ref)
     pass_weights(0)
     finish_filter(0, gf1_ref)
-    received(gw_all.at[part_blocks(1), :, 0:GROUP - 1], wr.at[3], friend)
+    received(gw_all[1].at[:, 0], wr.at[3], friend)
     turn(1)
     turn(2)
-    received(gw_all.at[part_blocks(0), :, 0:GROUP - 1], wr.at[2], friend)
+    received(gw_all[0].at[:, 0], wr.at[2], friend)
     turn(0)
     give(gb_o, gb_ref, 5)
     keep_plane.wait()
-    received(outg_ref.at[:, 0:GROUP - 1], or_.at[1], friend)
+    received(outg_ref.at[:, 0], or_.at[1], friend)
     sent(lev_ref.at[0, 0:ZN - 1], zs.at[0], friend)
     sent(lev_ref.at[0:GROUP - 1], gs.at[0], friend)
     sent(f1_ref.at[0:DP - 1], fs.at[0], friend)
     sent(f2_ref.at[0:DP - 1], fs.at[1], friend)
-    sent(cot_mid.at[0:ZN - 1], cs.at[0], friend)
-    sent(cot_ref.at[:, 0:GROUP - 1], cs.at[1], friend)
-    sent(out_mid.at[0:ZN - 1], os_.at[0], friend)
-    sent(outg_ref.at[:, 0:GROUP - 1], os_.at[1], friend)
+    sent(cot_mid.at[0:SEQ // 2 - 1], cs.at[0], friend)
+    sent(cot_ref.at[:, 0], cs.at[1], friend)
+    sent(out_mid.at[0:SEQ // 2 - 1], os_.at[0], friend)
+    sent(outg_ref.at[:, 0], os_.at[1], friend)
     for part in range(2):
         sent(gf_all.at[part, 0:DP - 1], hs.at[part], friend)
         sent(gw_in.at[0:DP - 1, part_rows(part)], ks.at[part], friend)
-        sent(gw_all.at[part_blocks(part), 0:ZN - 1, 0], ws.at[part], friend)
-        sent(gw_all.at[part_blocks(part), :, 0:GROUP - 1], ws.at[2 + part], friend)
+        sent(gw_all[part].at[0:SEQ // 2 - 1, 0], ws.at[part], friend)
+        sent(gw_all[part].at[:, 0], ws.at[2 + part], friend)
     for copy in gives:
         copy.wait()
 
@@ -513,7 +571,7 @@
     return pl.pallas_call(
         whole_kernel,
         out_shape=(
-            jax.ShapeDtypeStruct((ZN, GROUP, CH, TILE), bf16),
+            jax.ShapeDtypeStruct((SEQ // 2, 2, CH, TILE), bf16),
             jax.ShapeDtypeStruct((3, BINS), bf16),
             jax.ShapeDtypeStruct((3, BINS), bf16),
             jax.ShapeDtypeStruct((EVENTS, 3 * D), f32),
@@ -536,8 +594,8 @@
             vm((3 * D, EVENTS), f32),
             vm((COLS, EVENTS), bf16),
             vm((GROUP, ZN, EVENTS, TILE), bf16),
-            vm((ZN, GROUP, CH, TILE), bf16),
-            vm((ZN, GROUP, CH, TILE), bf16),
+            vm((SEQ // 2, 2, CH, TILE), bf16),
+            vm((SEQ // 2, 2, CH, TILE), bf16),
             vm((DP, CH, BINS // DP), bf16),
             vm((DP, CH, BINS // DP), bf16),
             vm((TILE, BINS), bf16),
@@ -560,13 +618,14 @@
             vm(spec, f32),
             vm(spec, f32),
             vm((COLS, BINS), bf16),
-            vm((ZN, GROUP, CH, TILE), bf16),
-            vm((ZN, GROUP, CH, TILE), bf16),
+            vm((SEQ // 2, 2, CH, TILE), bf16),
+            vm((SEQ // 2, 2, CH, TILE), bf16),
             vm((2, DP, SEQ, 3 * TILE), bf16),
-            vm((COLS, TILE), f32),
+            vm((40, TILE), f32),
             vm((2, DP, SEQ, 3 * TILE), bf16),
-            vm((DP, COLS, TILE), f32),
-            vm((3, ZN, GROUP, CH, TILE), bf16),
+            vm((DP, 40, TILE), f32),
+            vm((SEQ // 2, 2, 16, TILE), bf16),
+            vm((SEQ // 2, 2, 24, TILE), bf16),
             vm((8, BINS), f32),
             vm((2, 3, BINS), bf16),
             vm((EVENTS, 3 * D), f32),
@@ -575,11 +634,12 @@
             dma((6,)),
             dma((6,)),
             dma((8,)),
+            dma((8,)),
             dma((1,)),
             dma((1,)),
             dma((1,)),
             dma((2,)),
-            dma((2,)),
+            dma((4,)),
             dma((2,)),
             dma((2,)),
             dma((2,)),
@@ -624,7 +684,7 @@
 
 def body(counts, w_in, bias_one, bias_two, filter_one, filter_two, cotangent):
     out, gf1, gf2, gw, gb = whole(
-        counts[0].T, w_in, bias_one, bias_two, cotangent.reshape(ZN, GROUP, CH, TILE),
+        counts[0].T, w_in, bias_one, bias_two, cotangent.reshape(SEQ // 2, 2, CH, TILE),
         filter_one, filter_two,
     )
     out, gf1, gf2, gw, gb1, gb2 = finish(out.reshape(1, D, TILE), gf1, gf2, gw, gb)

time: 53.5 us -> 49.2 us (0.920)
  Pallas kernels: 52.7 us -> 48.5 us
    pallas_call x1, Pallas kernels: 50.7 us -> 46.4 us  [whole(): pl.pallas_call(whole_kernel, out_shape=(jax.ShapeDtypeStruct((SEQ // 2, 2...]
where the time goes in v4:
time: 49.2 us; the launch traced here: 49.1 us
  Pallas kernels  48.5 us (99%)
  between operations  0.64 us (1%)
    pallas_call x1, Pallas kernels, whole(): pl.pallas_call(whole_kernel, out_shape=(jax.ShapeDtypeStruct((SEQ // 2, 2...  46.4 us
    pallas_call x1, Pallas kernels, finish(): pl.pallas_call(finish_kernel, out_shape=(*like, flat, flat), in_specs=[VM...  2.05 us

profile of v4, /device:TPU:1, one launch (start us, length us, event | category | flops | bytes accessed | tf_op | source)
XLA Modules:
  0.0 49.1 jit_solution(7865808143077085483)
XLA Ops:
  0.6 46.4 %whole.1 = (bf16[16,2,24,128]{3,2,1,0:T(8,128)(2,1)}, bf16[3,4096]{1,0:T(4,128)(2,1)}, bf16[3,4096]{1,0:T(4,128)(2,1)}, f32[64,2304]{1,0:T(8,128)}, f32[2,768]{1,0:T(2,128)}) custom-call(s32[64,128]{1,0:T(8,128)} %bitcast.7, bf16[64,2304]{1,0:T(8,128)(2,1)} %w_in.1, f32[768]{0:T(1024)} %b1_in.1, f32[768]{0:T(1024)} %b2_in.1, ...), custom_call_target="tpu_custom_call" | custom-call | tf_op jit(solution)/shard_map/whole/pallas_call | solution.py:571
  47.1 2.1 %finish.1 = (bf16[1,768,128]{2,1,0:T(8,128)(2,1)}, bf16[3,4096]{1,0:T(4,128)(2,1)}, bf16[3,4096]{1,0:T(4,128)(2,1)}, f32[64,2304]{1,0:T(8,128)}, f32[768]{0:T(1024)}, /*index=5*/f32[768]{0:T(1024)}) custom-call(bf16[1,768,128]{2,1,0:T(8,128)(2,1)} %bitcast.6, bf16[3,4096]{1,0:T(4,128)(2,1)} %get-tuple-element.18.gf1_in, ...), custom_call_target="tpu_custom_call" | custom-call | tf_op jit(solution)/shard_map/finish/pallas_call | solution.py:675

commit v5 on v4

--- a/solution.py
+++ b/solution.py
@@ -113,7 +113,7 @@
     def hello(device):
         pl.semaphore_signal(barrier, inc=1, device_id=device, device_id_type=MESH)
 
-    for i in range(1, SEQ // 2):
+    for i in FAR:
         hello(same_core(s, i))
     hello(core_peer(s))
     for i in range(1, DP):
@@ -139,12 +139,12 @@
 
 def whole_kernel(
     counts_in, w_in, b1_in, b2_in, cot_in, f1_in, f2_in, table_in,
-    outg_ref, gf1_ref, gf2_ref, gwo_ref, gb_ref,
+    outg_ref, gf1_ref, gf2_ref, gwo_ref, gwv_ref,
     counts_ref, w_ref, table, b1_ref, b2_ref, w1_ref, w2_ref, v2_ref, v1_ref, tw_ref,
     own, wtt, wt_ref, lev_ref, cot_mid, cot_ref, f1_ref, f2_ref,
     levs, rows, crows, val, g1, g2, hid, gm, m1, m2, gh,
     tmp, inv, hat1, hat2, hatv, hath, hatg, hat_one_grad, gpb,
-    out_s, out_mid, gf_s, gwp, gf_all, gw_in, gw_v, gw_g, flat, gf_o, gw_o, gb_o,
+    out_s, out_mid, gf_s, gwp, gf_all, gw_in, gw_v, gw_g, flat, gf_o, gw_o,
     pre, loc, done, zr, xr, zs, gs, gr, fs, fr, cs, cr, os_, or_, hs, hr, ks, kr, ws, wr,
 ):
     s, d, z, q = place()
@@ -172,14 +172,8 @@
         return slice(c * SEQ, (c + 1) * SEQ)
 
     def put3(c, re, im):
-        rh, rl = split(re)
-        ih, il = split(im)
-        tmp[krows(c), 0:128] = rh
-        tmp[krows(c), 128:256] = ih
-        tmp[krows(c), 256:384] = rl
-        tmp[krows(c), 384:512] = il
-        tmp[krows(c), 512:640] = rh
-        tmp[krows(c), 640:768] = ih
+        tmp[krows(c), 0:128] = re.astype(bf16)
+        tmp[krows(c), 128:256] = im.astype(bf16)
 
     def forward(x_ref, dst):
         cr_ = tw_ref[0]
@@ -191,7 +185,7 @@
                 re = part[0:32, lanes(h)]
                 im = part[32:64, lanes(h)]
                 put3(2 * p + h, re * cr_ - im * ci_, re * ci_ + im * cr_)
-        dst[...] = dot(tmp[...], w2_ref[...])
+        dst[...] = dot(tmp[...], w2_ref[0:256, :]) + dot(tmp[...], w2_ref[256:512, :])
 
     def inverse(left, right, conj, emit):
         cr_ = tw_ref[0]
@@ -205,16 +199,16 @@
                 put3(c, lr * rr + li * ri, lr * ri - li * rr)
             else:
                 put3(c, lr * rr - li * ri, lr * ri + li * rr)
-        inv[...] = dot(tmp[...], v2_ref[...])
+        inv[...] = dot(tmp[...], v2_ref[0:256, :]) + dot(tmp[...], v2_ref[256:512, :])
         for p in range(CH // 2):
             cols = []
             for h in range(2):
                 c = 2 * p + h
                 re = inv[krows(c), 0:128]
                 im = inv[krows(c), 128:256]
-                rh, rl = split(re * cr_ + im * ci_)
-                ih, il = split(im * cr_ - re * ci_)
-                cols.append(jnp.concatenate([rh, ih, rl, il, rh, ih], axis=0))
+                rh = (re * cr_ + im * ci_).astype(bf16)
+                ih = (im * cr_ - re * ci_).astype(bf16)
+                cols.append(jnp.concatenate([rh, ih, rh, ih], axis=0))
             res = dot(v1_ref[...], jnp.concatenate(cols, axis=1))
             for h in range(2):
                 emit(2 * p + h, res[:, lanes(h)])
@@ -268,7 +262,8 @@
 
     def wg_copy(part):
         slot = gw_all[part].at[:, core]
-        return push(slot, slot, ws.at[2 + part], wr.at[2 + part], core_peer(s))
+        dst = gwv_ref.at[:, core] if part == 0 else slot
+        return push(slot, dst, ws.at[2 + part], wr.at[2 + part], core_peer(s))
 
     loads[0].wait()
     levels = jnp.log1p(counts_ref[...].astype(f32)) - 3.0
@@ -278,12 +273,12 @@
     for i in LINE:
         z_copy(i).start()
 
+    x_copy(0).start()
+    g_copy(0, 0).start()
+    fx_copy(f1_in, f1_ref, 0).start()
+    fx_copy(f2_in, f2_ref, 1).start()
     for i in FAR:
         far_copy(i, cot_in, cot_mid, 0, cs, cr).start()
-    fx_copy(f1_in, f1_ref, 0).start()
-    fx_copy(f2_in, f2_ref, 1).start()
-    x_copy(0).start()
-    g_copy(0, 0).start()
     for i in range(1, DP // 2):
         f_copy(i, f1_in, f1_ref, 0).start()
         f_copy(i, f2_in, f2_ref, 1).start()
@@ -305,12 +300,11 @@
     for at, ref in ((0, w2_ref), (256, v2_ref)):
         hi, lo = split(table[at:at + 256, :])
         ref[0:256, :] = hi
-        ref[256:512, :] = hi
-        ref[512:768, :] = lo
+        ref[256:512, :] = lo
     hi, lo = split(table[512:576, 0:32])
     w1_ref[...] = jnp.concatenate([hi, lo], axis=1)
     hi, lo = split(table[576:608, 0:64])
-    v1_ref[...] = jnp.concatenate([hi, hi, lo], axis=1)
+    v1_ref[...] = jnp.concatenate([hi, lo], axis=1)
     tw_ref[0] = table[608:640, 0:128]
     tw_ref[1] = table[608:640, 128:256]
 
@@ -503,19 +497,11 @@
         wz_copy(0, i).start()
 
     def turn(k):
-        low = lax.broadcasted_iota(jnp.int32, (8, TILE), 1) < EVENTS
         block = []
         for n in range(SEQ):
-            b = gw_all[min(k, 1)][n // 2, n % 2].astype(f32)
-            tiles = [b[r:r + 8] for r in range(0, b.shape[0], 8)]
-            if k == 0:
-                first, last = tiles
-                block.append(jnp.where(low, first, last))
-                block.append(
-                    jnp.where(low, pltpu.roll(first, EVENTS, 1), pltpu.roll(last, TILE - 1, 1))
-                )
-                block.append(jnp.where(low, last, pltpu.roll(last, TILE - 2, 1)))
-            elif k == 1:
+            b = gw_g[n // 2, n % 2].astype(f32)
+            tiles = [b[r:r + 8] for r in range(0, 24, 8)]
+            if k == 1:
                 block += [tiles[0], pltpu.roll(tiles[0], EVENTS, 1), tiles[1]]
             else:
                 block += [
@@ -523,13 +509,8 @@
                 ]
         for p in range(D // TILE):
             turned = jnp.concatenate(block[16 * p:16 * p + 16], axis=0).T
-            at = k * D + p * TILE
+            at = (k - 1) * D + p * TILE
             gw_o[:, at:at + TILE] = turned[0:EVENTS, :]
-            if k == 0:
-                gb_o[0:1, p * TILE:(p + 1) * TILE] = turned[EVENTS:EVENTS + 1, :]
-                gb_o[1:2, p * TILE:(p + 1) * TILE] = turned[EVENTS + 3:EVENTS + 4, :]
-        at = slice(k * D, (k + 1) * D)
-        give(gw_o.at[:, at], gwo_ref.at[:, at], 2 + k)
 
     def pass_weights(part):
         received(gw_all[part].at[0:SEQ // 2 - 1, 0], wr.at[part], friend)
@@ -537,14 +518,14 @@
 
     pass_weights(1)
     finish_filter(1, gf2_ref)
-    pass_weights(0)
-    finish_filter(0, gf1_ref)
     received(gw_all[1].at[:, 0], wr.at[3], friend)
     turn(1)
     turn(2)
-    received(gw_all[0].at[:, 0], wr.at[2], friend)
-    turn(0)
-    give(gb_o, gb_ref, 5)
+    give(gw_o, gwo_ref, 2)
+    pass_weights(0)
+    give(gw_v.at[:, core], gwv_ref.at[:, core], 3)
+    finish_filter(0, gf1_ref)
+    received(gw_v.at[:, 0], wr.at[2], friend)
     keep_plane.wait()
     received(outg_ref.at[:, 0], or_.at[1], friend)
     sent(lev_ref.at[0, 0:ZN - 1], zs.at[0], friend)
@@ -574,8 +555,8 @@
             jax.ShapeDtypeStruct((SEQ // 2, 2, CH, TILE), bf16),
             jax.ShapeDtypeStruct((3, BINS), bf16),
             jax.ShapeDtypeStruct((3, BINS), bf16),
-            jax.ShapeDtypeStruct((EVENTS, 3 * D), f32),
-            jax.ShapeDtypeStruct((2, D), f32),
+            jax.ShapeDtypeStruct((EVENTS, 2 * D), f32),
+            jax.ShapeDtypeStruct((SEQ // 2, 2, 16, TILE), bf16),
         ),
         in_specs=[ANY] * 8,
         out_specs=(ANY,) * 5,
@@ -586,9 +567,9 @@
             pltpu.SMEM((D,), f32),
             pltpu.SMEM((D,), f32),
             vm((2 * SEQ, 2 * SEQ), bf16),
-            vm((6 * TILE, 2 * TILE), bf16),
-            vm((6 * TILE, 2 * TILE), bf16),
-            vm((SEQ, 6 * SEQ), bf16),
+            vm((4 * TILE, 2 * TILE), bf16),
+            vm((4 * TILE, 2 * TILE), bf16),
+            vm((SEQ, 4 * SEQ), bf16),
             vm((2, SEQ, TILE), f32),
             vm((EVENTS, TILE), bf16),
             vm((3 * D, EVENTS), f32),
@@ -609,7 +590,7 @@
             vm((SEQ, LANES), f32),
             vm((SEQ, LANES), f32),
             vm((SEQ, LANES), bf16),
-            vm((SEQ * CH, 6 * TILE), bf16),
+            vm((SEQ * CH, 2 * TILE), bf16),
             vm(spec, f32),
             vm(spec, f32),
             vm(spec, f32),
@@ -628,8 +609,7 @@
             vm((SEQ // 2, 2, 24, TILE), bf16),
             vm((8, BINS), f32),
             vm((2, 3, BINS), bf16),
-            vm((EVENTS, 3 * D), f32),
-            vm((2, D), f32),
+            vm((EVENTS, 2 * D), f32),
             dma((5,)),
             dma((6,)),
             dma((6,)),
@@ -659,35 +639,54 @@
 
 
 def finish_kernel(
-    out_in, gf1_in, gf2_in, gw_in, gb_in, out_ref, gf1_ref, gf2_ref, gw_ref, gb1_ref, gb2_ref
+    out_in, gf1_in, gf2_in, gates_in, value_in,
+    out_ref, gf1_ref, gf2_ref, gw_ref, gb1_ref, gb2_ref,
 ):
+    low = lax.broadcasted_iota(jnp.int32, (8, TILE), 1) < EVENTS
+    block = []
+    for n in range(SEQ):
+        b = value_in[n // 2, n % 2].astype(f32)
+        first, last = b[0:8], b[8:16]
+        block.append(jnp.where(low, first, last))
+        block.append(
+            jnp.where(low, pltpu.roll(first, EVENTS, 1), pltpu.roll(last, TILE - 1, 1))
+        )
+        block.append(jnp.where(low, last, pltpu.roll(last, TILE - 2, 1)))
+    for p in range(D // TILE):
+        turned = jnp.concatenate(block[16 * p:16 * p + 16], axis=0).T
+        at = slice(p * TILE, (p + 1) * TILE)
+        gw_ref[:, at] = turned[0:EVENTS, :]
+        gb1_ref[at] = turned[EVENTS]
+        gb2_ref[at] = turned[EVENTS + 3]
+    gw_ref[:, D:] = gates_in[...]
     out_ref[...] = out_in[...]
     gf1_ref[...] = gf1_in[...]
     gf2_ref[...] = gf2_in[...]
-    gw_ref[...] = gw_in[...]
-    gb1_ref[...] = gb_in[0]
-    gb2_ref[...] = gb_in[1]
-
-
-def finish(out, gf1, gf2, gw, gb):
-    like = [jax.ShapeDtypeStruct(x.shape, x.dtype) for x in (out, gf1, gf2, gw)]
+
+
+def finish(out, gf1, gf2, gates, value):
+    def like(x):
+        return jax.ShapeDtypeStruct(x.shape, x.dtype)
+
     flat = jax.ShapeDtypeStruct((D,), f32)
     return pl.pallas_call(
         finish_kernel,
-        out_shape=(*like, flat, flat),
+        out_shape=(
+            like(out), like(gf1), like(gf2), jax.ShapeDtypeStruct((EVENTS, 3 * D), f32), flat, flat
+        ),
         in_specs=[VMEM] * 5,
         out_specs=(VMEM,) * 6,
         compiler_params=pltpu.CompilerParams(vmem_limit_bytes=LIMIT),
         name="finish",
-    )(out, gf1, gf2, gw, gb)
+    )(out, gf1, gf2, gates, value)
 
 
 def body(counts, w_in, bias_one, bias_two, filter_one, filter_two, cotangent):
-    out, gf1, gf2, gw, gb = whole(
+    out, gf1, gf2, gates, value = whole(
         counts[0].T, w_in, bias_one, bias_two, cotangent.reshape(SEQ // 2, 2, CH, TILE),
         filter_one, filter_two,
     )
-    out, gf1, gf2, gw, gb1, gb2 = finish(out.reshape(1, D, TILE), gf1, gf2, gw, gb)
+    out, gf1, gf2, gw, gb1, gb2 = finish(out.reshape(1, D, TILE), gf1, gf2, gates, value)
     return out, gw, gb1, gb2, gf1, gf2
 
 

time: 49.2 us -> 46.4 us (0.943)
  Pallas kernels: 48.5 us -> 45.6 us
    pallas_call x1, Pallas kernels: 46.4 us -> 43.4 us  [whole(): pl.pallas_call(whole_kernel, out_shape=(jax.ShapeDtypeStruct((SEQ // 2, 2...]
where the time goes in v5:
time: 46.4 us; the launch traced here: 46.2 us
  Pallas kernels  45.6 us (98%)
  between operations  0.64 us (1%)
    pallas_call x1, Pallas kernels, whole(): pl.pallas_call(whole_kernel, out_shape=(jax.ShapeDtypeStruct((SEQ // 2, 2...  43.4 us
    pallas_call x1, Pallas kernels, finish(): pl.pallas_call(finish_kernel, out_shape=(like(out), like(gf1), like(gf2),...  2.21 us

profile of v5, /device:TPU:1, one launch (start us, length us, event | category | flops | bytes accessed | tf_op | source)
XLA Modules:
  0.0 46.2 jit_solution(12026422558318439329)
XLA Ops:
  0.6 43.4 %whole.1 = (bf16[16,2,24,128]{3,2,1,0:T(8,128)(2,1)}, bf16[3,4096]{1,0:T(4,128)(2,1)}, bf16[3,4096]{1,0:T(4,128)(2,1)}, f32[64,1536]{1,0:T(8,128)}, bf16[16,2,16,128]{3,2,1,0:T(8,128)(2,1)}) custom-call(s32[64,128]{1,0:T(8,128)} %bitcast.7, bf16[64,2304]{1,0:T(8,128)(2,1)} %w_in.1, f32[768]{0:T(1024)} %b1_in.1, f32[768]{0:T(1024)} %b2_in.1, ...), custom_call_target="tpu_custom_call" | custom-call | tf_op jit(solution)/shard_map/whole/pallas_call | solution.py:552
  44.0 2.2 %finish.1 = (bf16[1,768,128]{2,1,0:T(8,128)(2,1)}, bf16[3,4096]{1,0:T(4,128)(2,1)}, bf16[3,4096]{1,0:T(4,128)(2,1)}, f32[64,2304]{1,0:T(8,128)}, f32[768]{0:T(1024)}, /*index=5*/f32[768]{0:T(1024)}) custom-call(bf16[1,768,128]{2,1,0:T(8,128)(2,1)} %bitcast.6, bf16[3,4096]{1,0:T(4,128)(2,1)} %get-tuple-element.18.gf1_in, ...), custom_call_target="tpu_custom_call" | custom-call | tf_op jit(solution)/shard_map/finish/pallas_call | solution.py:672

commit v6 on v5

--- a/solution.py
+++ b/solution.py
@@ -113,12 +113,13 @@
     def hello(device):
         pl.semaphore_signal(barrier, inc=1, device_id=device, device_id_type=MESH)
 
-    for i in FAR:
-        hello(same_core(s, i))
+    for i in LINE:
+        hello(z_peer(z, q, i))
+    hello(q_peer(z, q, 2))
     hello(core_peer(s))
     for i in range(1, DP):
         hello(dp_peer(d, i))
-    return lambda: pl.semaphore_wait(barrier, SEQ // 2 + DP - 1)
+    return lambda: pl.semaphore_wait(barrier, ZN + DP)
 
 
 def received(ref, sem, device):
@@ -278,7 +279,8 @@
     fx_copy(f1_in, f1_ref, 0).start()
     fx_copy(f2_in, f2_ref, 1).start()
     for i in FAR:
-        far_copy(i, cot_in, cot_mid, 0, cs, cr).start()
+        if i % 2 == 0:
+            far_copy(i, cot_in, cot_mid, 0, cs, cr).start()
     for i in range(1, DP // 2):
         f_copy(i, f1_in, f1_ref, 0).start()
         f_copy(i, f2_in, f2_ref, 1).start()
@@ -308,6 +310,11 @@
     tw_ref[0] = table[608:640, 0:128]
     tw_ref[1] = table[608:640, 128:256]
 
+    x_copy(0).wait_recv()
+    g_copy(2, 0).start()
+    for i in FAR:
+        if i % 2 == 1:
+            far_copy(i, cot_in, cot_mid, 0, cs, cr).start()
     for i in LINE:
         z_copy(i).wait_recv()
         x_copy(i).start()
@@ -316,7 +323,7 @@
         received(ref.at[0], fr.at[2 + k], friend)
         for j in range(1, DP // 2):
             fy_copy(j, ref, k).start()
-    for i in (0, *LINE):
+    for i in LINE:
         x_copy(i).wait_recv()
         g_copy(2, i).start()
 
@@ -363,28 +370,27 @@
     inverse(hat1, hatv, False, emit_one)
     forward(hid, hath)
 
-    keep_cot.wait()
-    received(cot_ref.at[:, 0], cr.at[1], friend)
-    for a in range(SEQ):
-        crows[a * CH:(a + 1) * CH, :] = cot_ref[a // 2, a % 2].astype(f32)
-
     def emit_two(c, conv):
         mixed = rnd(conv) + b2_ref[base + c] * hid[:, lanes(c)].astype(f32)
-        up = crows[pl.ds(c, SEQ, stride=CH), :] * scale
-        gate = g2[:, lanes(c)].astype(f32)
-        rows[pl.ds(2 * CH + c, SEQ, stride=COLS), :] = up * mixed
-        m2[:, lanes(c)] = gate * mixed
-        gm[:, lanes(c)] = (up * gate).astype(bf16)
+        m2[:, lanes(c)] = mixed
+        crows[pl.ds(c, SEQ, stride=CH), :] = g2[:, lanes(c)].astype(f32) * mixed
 
     inverse(hat2, hath, False, emit_two)
-    for c in range(CH):
-        crows[pl.ds(c, SEQ, stride=CH), :] = m2[:, lanes(c)]
     for a in range(SEQ):
         out_s[a // 2, a % 2] = crows[a * CH:(a + 1) * CH, :].astype(bf16)
     for i in FAR:
         far_copy(i, out_s, out_mid, 0, os_, or_).start()
     keep_out = pltpu.make_async_copy(out_s.at[m], out_mid.at[m], loc.at[4])
     keep_out.start()
+
+    keep_cot.wait()
+    received(cot_ref.at[:, 0], cr.at[1], friend)
+    for a in range(SEQ):
+        crows[a * CH:(a + 1) * CH, :] = cot_ref[a // 2, a % 2].astype(f32)
+    for c in range(CH):
+        up = crows[pl.ds(c, SEQ, stride=CH), :] * scale
+        rows[pl.ds(2 * CH + c, SEQ, stride=COLS), :] = up * m2[:, lanes(c)]
+        gm[:, lanes(c)] = (up * g2[:, lanes(c)].astype(f32)).astype(bf16)
 
     def bias_sums(x_ref, y_ref):
         parts = []

time: 46.4 us -> 44.6 us (0.961)
  Pallas kernels: 45.6 us -> 43.9 us
    pallas_call x1, Pallas kernels: 43.4 us -> 41.6 us  [whole(): pl.pallas_call(whole_kernel, out_shape=(jax.ShapeDtypeStruct((SEQ // 2, 2...]
where the time goes in v6:
time: 44.6 us; the launch traced here: 44.5 us
  Pallas kernels  43.9 us (98%)
  between operations  0.64 us (1%)
    pallas_call x1, Pallas kernels, whole(): pl.pallas_call(whole_kernel, out_shape=(jax.ShapeDtypeStruct((SEQ // 2, 2...  41.6 us
    pallas_call x1, Pallas kernels, finish(): pl.pallas_call(finish_kernel, out_shape=(like(out), like(gf1), like(gf2),...  2.21 us

profile of v6, /device:TPU:1, one launch (start us, length us, event | category | flops | bytes accessed | tf_op | source)
XLA Modules:
  0.0 44.5 jit_solution(5329467003530454401)
XLA Ops:
  0.6 41.6 %whole.1 = (bf16[16,2,24,128]{3,2,1,0:T(8,128)(2,1)}, bf16[3,4096]{1,0:T(4,128)(2,1)}, bf16[3,4096]{1,0:T(4,128)(2,1)}, f32[64,1536]{1,0:T(8,128)}, bf16[16,2,16,128]{3,2,1,0:T(8,128)(2,1)}) custom-call(s32[64,128]{1,0:T(8,128)} %bitcast.7, bf16[64,2304]{1,0:T(8,128)(2,1)} %w_in.1, f32[768]{0:T(1024)} %b1_in.1, f32[768]{0:T(1024)} %b2_in.1, ...), custom_call_target="tpu_custom_call" | custom-call | tf_op jit(solution)/shard_map/whole/pallas_call | solution.py:558
  42.3 2.2 %finish.1 = (bf16[1,768,128]{2,1,0:T(8,128)(2,1)}, bf16[3,4096]{1,0:T(4,128)(2,1)}, bf16[3,4096]{1,0:T(4,128)(2,1)}, f32[64,2304]{1,0:T(8,128)}, f32[768]{0:T(1024)}, /*index=5*/f32[768]{0:T(1024)}) custom-call(bf16[1,768,128]{2,1,0:T(8,128)(2,1)} %bitcast.6, bf16[3,4096]{1,0:T(4,128)(2,1)} %get-tuple-element.18.gf1_in, ...), custom_call_target="tpu_custom_call" | custom-call | tf_op jit(solution)/shard_map/finish/pallas_call | solution.py:678

commit v7 on v6

--- a/solution.py
+++ b/solution.py
@@ -492,15 +492,15 @@
     for i in range(1, DP):
         h_copy(0, i).start()
 
+    received(gw_in.at[0:DP - 1, part_rows(0)], kr.at[0], friend)
+    total_rows(0)
+    for i in FAR:
+        wz_copy(0, i).start()
     keep_out.wait()
     received(out_mid.at[0:SEQ // 2 - 1], or_.at[0], friend)
     near_copy(out_mid, outg_ref, 1, os_, or_).start()
     keep_plane = pltpu.make_async_copy(out_mid.at[:, core], outg_ref.at[:, core], loc.at[5])
     keep_plane.start()
-    received(gw_in.at[0:DP - 1, part_rows(0)], kr.at[0], friend)
-    total_rows(0)
-    for i in FAR:
-        wz_copy(0, i).start()
 
     def turn(k):
         block = []

time: 44.6 us -> 44.6 us (level)
  no operation moved by 1% of the time
where the time goes in v7:
time: 44.6 us; the launch traced here: 44.5 us
  Pallas kernels  43.9 us (98%)
  between operations  0.64 us (1%)
    pallas_call x1, Pallas kernels, whole(): pl.pallas_call(whole_kernel, out_shape=(jax.ShapeDtypeStruct((SEQ // 2, 2...  41.6 us
    pallas_call x1, Pallas kernels, finish(): pl.pallas_call(finish_kernel, out_shape=(like(out), like(gf1), like(gf2),...  2.21 us

profile of v7, /device:TPU:1, one launch (start us, length us, event | category | flops | bytes accessed | tf_op | source)
XLA Modules:
  0.0 44.5 jit_solution(12279773215522475987)
XLA Ops:
  0.6 41.6 %whole.1 = (bf16[16,2,24,128]{3,2,1,0:T(8,128)(2,1)}, bf16[3,4096]{1,0:T(4,128)(2,1)}, bf16[3,4096]{1,0:T(4,128)(2,1)}, f32[64,1536]{1,0:T(8,128)}, bf16[16,2,16,128]{3,2,1,0:T(8,128)(2,1)}) custom-call(s32[64,128]{1,0:T(8,128)} %bitcast.7, bf16[64,2304]{1,0:T(8,128)(2,1)} %w_in.1, f32[768]{0:T(1024)} %b1_in.1, f32[768]{0:T(1024)} %b2_in.1, ...), custom_call_target="tpu_custom_call" | custom-call | tf_op jit(solution)/shard_map/whole/pallas_call | solution.py:558
  42.3 2.2 %finish.1 = (bf16[1,768,128]{2,1,0:T(8,128)(2,1)}, bf16[3,4096]{1,0:T(4,128)(2,1)}, bf16[3,4096]{1,0:T(4,128)(2,1)}, f32[64,2304]{1,0:T(8,128)}, f32[768]{0:T(1024)}, /*index=5*/f32[768]{0:T(1024)}) custom-call(bf16[1,768,128]{2,1,0:T(8,128)(2,1)} %bitcast.6, bf16[3,4096]{1,0:T(4,128)(2,1)} %get-tuple-element.18.gf1_in, ...), custom_call_target="tpu_custom_call" | custom-call | tf_op jit(solution)/shard_map/finish/pallas_call | solution.py:678
